TPU v7x, 128 devices: a whole 4x4x4 slice. The times are simulated.
128 devices in a mesh: section: 4 (over z), shard: 32 (over y, x, core).
Axes of the slice: x: 4, y: 4, z: 4, core: 2. Of those that a mesh axis runs over, the one named last changes fastest.
Arguments:
- saved: bfloat16 [4, 4, 1024, 8, 1024], P('section', None, 'shard'), may hold values from -6 to 6
- pooled: bfloat16 [4, 1024, 8, 1024], P('section', 'shard'), may hold values from -6 to 6
- grad_top: bfloat16 [4, 1024, 8, 1024], P(None, 'shard'), may hold values from -6 to 6
- w_in: bfloat16 [4, 1024, 1024], P('section'), may hold values from -0.1875 to 0.1875
- w_out: bfloat16 [4, 1024, 1024], P('section'), may hold values from -0.1875 to 0.1875
- feature_ids: int32 [4, 1024, 8], P(None, 'shard'), may hold values from 0 to 131071, as said below
- holder_order: int32 [4], replicated, may hold values from 0 to 3, each once
Outputs:
- grad_w_in: float32 [4, 1024, 1024], P('section', 'shard')
- grad_w_out: float32 [4, 1024, 1024], P('section', 'shard')
- table_grad: float32 [131072, 1024], P(('section', 'shard'))
Inputs may be any that keep to these rules, and one draw needn't show every extreme that they name: `feature_ids`: feature k names a row of table k, rows k * 16384 to (k + 1) * 16384 - 1. Row i belongs to owner i // 1024. In each micro-batch, the rows j * 32 to (j + 1) * 32 - 1 name exactly 2 rows of every owner.
All inputs are finite; a program needn't handle non-finite values.
Results may differ from a plain program's by a relative error of at most 0.0095.
Values may be sent and summed in bfloat16 or wider, within the bound.
A program may use at most 192 MiB of HBM per device.

v0:
```python
import jax
import jax.numpy as jnp
from jax import lax
from jax.experimental import pallas as pl
from jax.experimental.pallas import tpu as pltpu
from jax.sharding import PartitionSpec as P

ROWS_OWN = 1024
MESH = pl.DeviceIdType.MESH
F32 = jnp.float32
BF16 = jnp.bfloat16

SECTIONS = 4
SHARDS = 32
SIDE = 4
MICRO = 4
TOK = 256
CHUNK = 128
WIDTH = 1024
SHARE = WIDTH // SHARDS
PER_PLANE = TOK // SECTIONS
TILE = 256
CHUNKS = TOK // CHUNK


def dot_nt(a, b):
    return lax.dot_general(a, b, (((1,), (1,)), ((), ())), preferred_element_type=F32)


def dot_tn(a, b):
    return lax.dot_general(a, b, (((0,), (0,)), ((), ())), preferred_element_type=F32)


def kernel(
    inverse,
    saved,
    pooled,
    grad_top,
    w_in,
    w_out,
    rank,
    out_in,
    out_out,
    out_rows,
    win,
    wout,
    xbuf,
    gbuf,
    nbuf,
    pbuf,
    act,
    slope,
    dz,
    acc,
    sorted_rows,
    routed,
    spread,
    send_a,
    recv_a,
    send_b,
    recv_b,
    own_b,
    send_c,
    recv_c,
    load_sem,
    top_sem,
    pool_send,
    pool_recv,
    relay_send,
    relay_recv,
    route_send,
    route_recv,
    spread_send,
    spread_recv,
    a_send,
    a_recv,
    b_send,
    b_recv,
    c_send,
    c_recv,
):
    sec = lax.axis_index("section")
    sh = lax.axis_index("shard")
    core = sh % 2
    px = (sh // 2) % SIDE
    py = sh // (2 * SIDE)
    first = sec == 0
    last = sec == SECTIONS - 1

    def at(y, x, c):
        return (sec, (y * SIDE + x) * 2 + c)

    def micro_rows(m):
        return pl.ds(pl.multiple_of(m * TOK, TOK), TOK)

    def chunk_rows(c):
        return pl.ds(pl.multiple_of(c * CHUNK, CHUNK), CHUNK)

    def load_x(m):
        rows = micro_rows(m)
        return pltpu.make_async_copy(saved.at[rows], xbuf.at[rows], load_sem.at[2 + m])

    def load_top(m):
        rows = micro_rows(m)
        return pltpu.make_async_copy(grad_top.at[rows], gbuf.at[rows], top_sem.at[m])

    load_win = pltpu.make_async_copy(w_in, win, load_sem.at[0])
    load_wout = pltpu.make_async_copy(w_out, wout, load_sem.at[1])
    load_pool = pltpu.make_async_copy(pooled, pbuf.at[0], load_sem.at[2 + MICRO])

    load_win.start()
    load_x(0).start()
    load_wout.start()

    @pl.when(last)
    def _():
        for m in range(MICRO):
            load_top(m).start()

    for m in range(1, MICRO):
        load_x(m).start()

    @pl.when(first)
    def _():
        load_pool.start()

    barrier = pltpu.get_barrier_semaphore()

    def greet(k, carry):
        pl.semaphore_signal(
            barrier, inc=1, device_id=(sec, (sh + k) % SHARDS), device_id_type=MESH
        )
        return carry

    lax.fori_loop(1, SHARDS, greet, 0)
    for k in range(1, SECTIONS):
        pl.semaphore_signal(
            barrier, inc=1, device_id=((sec + k) % SECTIONS, sh), device_id_type=MESH
        )
    pl.semaphore_wait(barrier, SHARDS - 1 + SECTIONS - 1)

    def pool_copy(s):
        return pltpu.make_async_remote_copy(
            src_ref=pooled,
            dst_ref=pbuf.at[s],
            send_sem=pool_send,
            recv_sem=pool_recv.at[s],
            device_id=(0, sh),
            device_id_type=MESH,
        )

    def relay_copy(c):
        rows = chunk_rows(c)
        return pltpu.make_async_remote_copy(
            src_ref=nbuf.at[rows],
            dst_ref=gbuf.at[rows],
            send_sem=relay_send.at[c],
            recv_sem=relay_recv.at[c],
            device_id=(jnp.maximum(sec - 1, 0), sh),
            device_id_type=MESH,
        )

    def route_copy(m, p):
        return pltpu.make_async_remote_copy(
            src_ref=sorted_rows.at[m, pl.ds(p * PER_PLANE, PER_PLANE)],
            dst_ref=routed.at[pl.ds(pl.multiple_of(m * PER_PLANE, PER_PLANE), PER_PLANE)],
            send_sem=route_send.at[m, p],
            recv_sem=route_recv.at[m],
            device_id=(p, sh),
            device_id_type=MESH,
        )

    @pl.when(jnp.logical_not(first))
    def _():
        pool_copy(sec).start()

    def clear(i, carry):
        rows = pl.ds(pl.multiple_of(i * 64, 64), 64)
        for mat in range(2):
            acc[mat, rows, :] = jnp.zeros((64, WIDTH), F32)
        return carry

    lax.fori_loop(0, WIDTH // 64, clear, 0)

    load_win.wait()

    def micro_step(m, carry):
        rows = micro_rows(m)
        load_x(m).wait()

        @pl.when(first)
        def _():
            @pl.when(m == 0)
            def _():
                load_pool.wait()
                for s in range(1, SECTIONS):
                    pool_copy(s).wait_recv()

            extra = pbuf[inverse[m]]
            xbuf[rows, :] = (xbuf[rows, :].astype(F32) + extra.astype(F32)).astype(BF16)

        for j in range(WIDTH // TILE):
            cols = pl.ds(j * TILE, TILE)
            z = jnp.dot(xbuf[rows, :], win[:, cols], preferred_element_type=F32)
            sig = jax.nn.sigmoid(z)
            act[:, cols] = (z * sig).astype(BF16)
            slope[:, cols] = sig * (1.0 + z * (1.0 - sig))

        @pl.when(m == 0)
        def _():
            load_wout.wait()

        @pl.when(last)
        def _():
            load_top(m).wait()

        for k in range(CHUNKS):
            c = m * CHUNKS + k
            crows = chunk_rows(c)
            krows = pl.ds(k * CHUNK, CHUNK)

            @pl.when(jnp.logical_not(last))
            def _():
                relay_copy(c).wait_recv()

            g = gbuf[crows, :]
            for j in range(WIDTH // TILE):
                cols = pl.ds(j * TILE, TILE)
                ga = dot_nt(g, wout[cols, :])
                dz[krows, cols] = (ga * slope[krows, cols]).astype(BF16)
            for j in range(WIDTH // TILE):
                cols = pl.ds(j * TILE, TILE)
                back = dot_nt(dz[krows, :], win[cols, :])
                nbuf[crows, cols] = (gbuf[crows, cols].astype(F32) + back).astype(BF16)

            @pl.when(jnp.logical_not(first))
            def _():
                relay_copy(c).start()

        @pl.when(first)
        def _():
            target = lax.broadcasted_iota(jnp.int32, (TOK, TOK), 0)
            pick = jnp.where(target == rank[m], 1.0, 0.0).astype(BF16)
            ordered = jnp.dot(pick, nbuf[rows, :], preferred_element_type=F32).astype(BF16)
            sorted_rows[m] = ordered
            for p in range(1, SECTIONS):
                route_copy(m, p).start()
            routed[pl.ds(pl.multiple_of(m * PER_PLANE, PER_PLANE), PER_PLANE), :] = ordered[
                :PER_PLANE, :
            ]

        def weight_tile(i, inner):
            cols = pl.ds(pl.multiple_of(i * TILE, TILE), TILE)
            acc[0, cols, :] += dot_tn(xbuf[rows, cols], dz[...])
            acc[1, cols, :] += dot_tn(act[:, cols], gbuf[rows, :])
            return inner

        lax.fori_loop(0, WIDTH // TILE, weight_tile, 0)
        return carry

    lax.fori_loop(0, MICRO, micro_step, 0)

    def mine(mat):
        return px if mat == 0 else py

    def acc_rows(mat, t, o, c):
        block = (o * SIDE + t) if mat == 0 else (t * SIDE + o)
        return pl.ds(pl.multiple_of(block * 2 * SHARE + c * SHARE, SHARE), SHARE)

    def a_copy(mat, t):
        return pltpu.make_async_remote_copy(
            src_ref=send_a.at[mat, t],
            dst_ref=recv_a.at[mat, t],
            send_sem=a_send.at[mat, t],
            recv_sem=a_recv.at[mat, t],
            device_id=at(py, px, 1 - core),
            device_id_type=MESH,
        )

    def b_copy(mat, d):
        t = (mine(mat) + d) % SIDE
        return pltpu.make_async_remote_copy(
            src_ref=send_b.at[mat, d - 1],
            dst_ref=recv_b.at[mat, d - 1],
            send_sem=b_send.at[mat, d - 1],
            recv_sem=b_recv.at[mat, d - 1],
            device_id=at(py, t, core) if mat == 0 else at(t, px, core),
            device_id_type=MESH,
        )

    def c_copy(mat, d):
        t = (mine(1 - mat) + d) % SIDE
        return pltpu.make_async_remote_copy(
            src_ref=send_c.at[mat, d - 1],
            dst_ref=recv_c.at[mat, d - 1],
            send_sem=c_send.at[mat, d - 1],
            recv_sem=c_recv.at[mat, d - 1],
            device_id=at(t, px, core) if mat == 0 else at(py, t, core),
            device_id_type=MESH,
        )

    order = (2, 1, 3, 0)
    for d in order:
        for mat in range(2):
            t = (mine(mat) + d) % SIDE

            def fill_a(o, carry, mat=mat, t=t):
                send_a[mat, t, o] = acc[mat, acc_rows(mat, t, o, 1 - core), :].astype(BF16)
                return carry

            lax.fori_loop(0, SIDE, fill_a, 0)
            a_copy(mat, t).start()

    for d in order:
        for mat in range(2):
            t = (mine(mat) + d) % SIDE
            a_copy(mat, t).wait_recv()

            def add_a(o, carry, mat=mat, t=t, d=d):
                both = acc[mat, acc_rows(mat, t, o, core), :] + recv_a[mat, t, o].astype(F32)
                if d == 0:
                    own_b[mat, o] = both
                else:
                    send_b[mat, d - 1, o] = both.astype(BF16)
                return carry

            lax.fori_loop(0, SIDE, add_a, 0)
            if d != 0:
                b_copy(mat, d).start()

    @pl.when(jnp.logical_not(first))
    def _():
        for m in range(MICRO):
            route_copy(m, 1).wait_recv()

    row = lax.broadcasted_iota(jnp.int32, (TOK, TOK), 0)
    col = lax.broadcasted_iota(jnp.int32, (TOK, TOK), 1)
    source = ((row >> 1) & 3) * PER_PLANE + (row >> 3) * 2 + (row & 1)
    regroup = jnp.where(source == col, 1.0, 0.0).astype(BF16)
    by_owner = jnp.dot(regroup, routed[...], preferred_element_type=F32)
    spread[...] = by_owner.reshape(SHARDS, 2 * MICRO, WIDTH).astype(BF16)

    def spread_copy(k, to, came):
        return pltpu.make_async_remote_copy(
            src_ref=spread.at[to],
            dst_ref=out_rows.at[came],
            send_sem=spread_send.at[k],
            recv_sem=spread_recv.at[k],
            device_id=(sec, to),
            device_id_type=MESH,
        )

    def hand_out(k, carry):
        spread_copy(k, (sh + k) % SHARDS, sh).start()
        return carry

    lax.fori_loop(1, SHARDS, hand_out, 0)
    out_rows[sh] = spread[sh]

    for d in range(1, SIDE):
        for mat in range(2):
            b_copy(mat, d).wait_recv()
    for mat in range(2):

        def add_b(o, carry, mat=mat):
            total = own_b[mat, o]
            for d in range(1, SIDE):
                total = total + recv_b[mat, d - 1, o].astype(F32)
            own_b[mat, o] = total
            return carry

        lax.fori_loop(0, SIDE, add_b, 0)
        for d in (2, 1, 3):
            t = (mine(1 - mat) + d) % SIDE
            send_c[mat, d - 1] = own_b[mat, t].astype(BF16)
            c_copy(mat, d).start()

    for mat, out in ((0, out_in), (1, out_out)):
        total = own_b[mat, mine(1 - mat)]
        for d in range(1, SIDE):
            c_copy(mat, d).wait_recv()
            total = total + recv_c[mat, d - 1].astype(F32)
        out[...] = total

    def collect(k, carry):
        spread_copy(k, (sh + k) % SHARDS, (sh + SHARDS - k) % SHARDS).wait_recv()
        return carry

    lax.fori_loop(1, SHARDS, collect, 0)

    @pl.when(jnp.logical_not(first))
    def _():
        pool_copy(sec).wait_send()

        def left(c, carry):
            relay_copy(c).wait_send()
            return carry

        lax.fori_loop(0, MICRO * CHUNKS, left, 0)

    @pl.when(first)
    def _():
        for m in range(MICRO):
            for p in range(1, SECTIONS):
                route_copy(m, p).wait_send()

    def spread_left(k, carry):
        spread_copy(k, (sh + k) % SHARDS, sh).wait_send()
        return carry

    lax.fori_loop(1, SHARDS, spread_left, 0)
    for mat in range(2):
        for t in range(SIDE):
            a_copy(mat, t).wait_send()
        for d in range(1, SIDE):
            b_copy(mat, d).wait_send()
            c_copy(mat, d).wait_send()


def relay(inverse, saved, pooled, grad_top, w_in, w_out, rank):
    vmem = pl.BlockSpec(memory_space=pltpu.VMEM)
    anywhere = pl.BlockSpec(memory_space=pl.ANY)
    dma = pltpu.SemaphoreType.DMA
    tokens = MICRO * TOK
    return pl.pallas_call(
        kernel,
        out_shape=(
            jax.ShapeDtypeStruct((SHARE, WIDTH), F32),
            jax.ShapeDtypeStruct((SHARE, WIDTH), F32),
            jax.ShapeDtypeStruct((SHARDS, 2 * MICRO, WIDTH), BF16),
        ),
        in_specs=[pl.BlockSpec(memory_space=pltpu.SMEM)] + [anywhere] * 5 + [vmem],
        out_specs=(vmem, vmem, vmem),
        scratch_shapes=[
            pltpu.VMEM((WIDTH, WIDTH), BF16),
            pltpu.VMEM((WIDTH, WIDTH), BF16),
            pltpu.VMEM((tokens, WIDTH), BF16),
            pltpu.VMEM((tokens, WIDTH), BF16),
            pltpu.VMEM((tokens, WIDTH), BF16),
            pltpu.VMEM((SECTIONS, TOK, WIDTH), BF16),
            pltpu.VMEM((TOK, WIDTH), BF16),
            pltpu.VMEM((TOK, WIDTH), F32),
            pltpu.VMEM((TOK, WIDTH), BF16),
            pltpu.VMEM((2, WIDTH, WIDTH), F32),
            pltpu.VMEM((MICRO, TOK, WIDTH), BF16),
            pltpu.VMEM((TOK, WIDTH), BF16),
            pltpu.VMEM((SHARDS, 2 * MICRO, WIDTH), BF16),
            pltpu.VMEM((2, SIDE, SIDE, SHARE, WIDTH), BF16),
            pltpu.VMEM((2, SIDE, SIDE, SHARE, WIDTH), BF16),
            pltpu.VMEM((2, SIDE - 1, SIDE, SHARE, WIDTH), BF16),
            pltpu.VMEM((2, SIDE - 1, SIDE, SHARE, WIDTH), BF16),
            pltpu.VMEM((2, SIDE, SHARE, WIDTH), F32),
            pltpu.VMEM((2, SIDE - 1, SHARE, WIDTH), BF16),
            pltpu.VMEM((2, SIDE - 1, SHARE, WIDTH), BF16),
            dma((3 + MICRO,)),
            dma((MICRO,)),
            dma,
            dma((SECTIONS,)),
            dma((MICRO * CHUNKS,)),
            dma((MICRO * CHUNKS,)),
            dma((MICRO, SECTIONS)),
            dma((MICRO,)),
            dma((SHARDS,)),
            dma((SHARDS,)),
            dma((2, SIDE)),
            dma((2, SIDE)),
            dma((2, SIDE - 1)),
            dma((2, SIDE - 1)),
            dma((2, SIDE - 1)),
            dma((2, SIDE - 1)),
        ],
        compiler_params=pltpu.CompilerParams(
            collective_id=0, has_side_effects=True, vmem_limit_bytes=56 * 1024 * 1024
        ),
        cost_estimate=pl.CostEstimate(
            flops=10 * tokens * WIDTH * WIDTH, bytes_accessed=9 * 2**20, transcendentals=tokens * WIDTH
        ),
        name="relay",
    )(inverse, saved, pooled, grad_top, w_in, w_out, rank)


def local(saved, pooled, grad_top, w_in, w_out, feature_ids, holder_order):
    section_id = lax.axis_index("section")
    shard_id = lax.axis_index("shard")
    tokens = MICRO * TOK
    micro_range = jnp.arange(MICRO, dtype=jnp.int32)
    inverse = jnp.sum(
        jnp.where(holder_order[None, :] == micro_range[:, None], micro_range[None, :], 0), axis=1
    )
    ids = feature_ids.reshape(MICRO, TOK)
    owner = ids // ROWS_OWN
    position = jnp.arange(TOK, dtype=jnp.int32)
    earlier = (owner[:, :, None] == owner[:, None, :]) & (position[None, :] < position[:, None])
    rank = 2 * owner + jnp.sum(earlier.astype(jnp.int32), axis=2)
    out_in, out_out, rows = relay(
        inverse,
        saved.reshape(tokens, WIDTH),
        pooled.reshape(TOK, WIDTH),
        grad_top.reshape(tokens, WIDTH),
        w_in[0],
        w_out[0],
        rank.reshape(MICRO, 1, TOK),
    )
    all_ids = lax.all_gather(ids, "shard", axis=0)
    own = section_id * SHARDS + shard_id
    key = position * ROWS_OWN + all_ids % ROWS_OWN
    named = all_ids // ROWS_OWN == own
    low = jnp.min(jnp.where(named, key, TOK * ROWS_OWN), axis=2)
    high = jnp.max(jnp.where(named, key, -1), axis=2)
    row_of = (jnp.stack([low, high], axis=2) % ROWS_OWN).reshape(-1)
    one_hot = (jnp.arange(ROWS_OWN, dtype=jnp.int32)[:, None] == row_of[None, :]).astype(BF16)
    table_grad = jnp.dot(one_hot, rows.reshape(-1, WIDTH), preferred_element_type=F32)
    return (out_in[None], out_out[None], table_grad)


def solution(mesh):
    return jax.shard_map(
        local,
        mesh=mesh,
        in_specs=(
            P("section", None, "shard", None, None),
            P("section", "shard", None, None),
            P(None, "shard", None, None),
            P("section", None, None),
            P("section", None, None),
            P(None, "shard", None),
            P(),
        ),
        out_specs=(
            P("section", "shard", None),
            P("section", "shard", None),
            P(("section", "shard"), None),
        ),
        check_vma=False,
    )
```

profile of v0, /device:TPU:1, one launch (start us, length us, event | category | flops | bytes accessed | tf_op | source)
XLA Modules:
  0.0 140.1 jit_solution(9414295867390265173)
XLA Ops:
  0.6 1.3 select_reduce_fusion.2.inverse
  1.9 0.8 copy.29
  2.7 0.1 all_gather_reshape.3
  2.8 0.1 reshape.183
  2.9 0.1 reshape.185
  3.1 0.4 convert_reduce_fusion
  3.5 0.6 reshape_add_fusion.rank
  4.1 26.2 %all_gather.3 = s32[32,4,256]{2,1,0:T(4,128)S(1)} all-gather(s32[1,4,256]{2,1,0:T(4,128)S(1)} %all_gather_reshape.3), channel_id=1, replica_groups=mesh['section'=4,'shard'=32] {'shard'}, dimensions={0}, use_global_device_ids=true | all-gather | bytes 135168 | tf_op jit(solution)/shard_map/all_gather | solution.py:504
  30.3 1.2 select_reduce_fusion.1
  31.5 0.1 copy.36
  31.6 0.1 copy.37
  31.6 0.1 copy.38
  31.8 0.2 stack.14
  31.9 103.0 %relay.1 = (f32[32,1024]{1,0:T(8,128)}, f32[32,1024]{1,0:T(8,128)}, bf16[32,8,1024]{2,1,0:T(8,128)(2,1)}) custom-call(s32[4]{0:T(128)} %select_reduce_fusion.2.inverse, bf16[1024,1024]{1,0:T(8,128)(2,1)} %bitcast.16, bf16[256,1024]{1,0:T(8,128)(2,1)} %bitcast.20, bf16[1024,1024]{1,0:T(8,128)(2,1)} %bitcast.17, bf16[1024,1024]{1,0:T(8,128)(2,1)} %bitcast.18, ...), custom_call_target="tpu_custom_call" | custom-call | flops 10737418240 | bytes 9437184 | tf_op jit(solution)/shard_map/relay/pallas_call | solution.py:425
  135.0 0.0 copy-start.1
  135.0 0.0 copy-start
  135.0 3.8 %fusion = f32[1024,1024]{1,0:T(8,128)} fusion(bf16[32,8,1024]{2,1,0:T(8,128)(2,1)} %get-tuple-element.8, s32[256]{0:T(256)S(1)} %and_select_fusion.1), kind=kOutput, calls=%fused_computation.2 | convolution fusion | flops 537133056 | bytes 4719616 | tf_op jit(solution)/shard_map/dot_general | solution.py:512
  138.8 0.0 copy-done.1
  138.8 0.7 copy.41
  139.5 0.0 copy-done
  139.5 0.7 copy.42
  (5 shorter events, 0.1 us)
Async XLA Ops:
  135.0 3.8 %copy-start.1 = (f32[32,1024]{1,0:T(8,128)S(1)}, f32[32,1024]{1,0:T(8,128)}, u32[]{:S(2)}) copy-start(f32[32,1024]{1,0:T(8,128)} %get-tuple-element.6) | copy-start | bytes 393220
  135.0 4.5 %copy-start = (f32[32,1024]{1,0:T(8,128)S(1)}, f32[32,1024]{1,0:T(8,128)}, u32[]{:S(2)}) copy-start(f32[32,1024]{1,0:T(8,128)} %get-tuple-element.7) | copy-start | bytes 393220
where the time goes:
time: 140 us
  Pallas kernels  103 us (74%)
  blocking collectives  26.2 us (19%)
  matrix products  3.81 us (3%)
  other arithmetic  3.53 us (3%)
  local copies, waits for them, and re-layouts  2.83 us (2%)
    pallas_call x1, Pallas kernels, relay(): pl.pallas_call(kernel, out_shape=(jax.ShapeDtypeStruct((SHARE, WIDTH), F3...  103 us
    all_gather x1, blocking collectives, local(): all_ids = lax.all_gather(ids, 'shard', axis=0)  26.2 us
    dot_general x1, matrix products, local(): jnp.dot(one_hot, rows.reshape(-1, WIDTH), preferred_element_type=F32)  3.81 us

commit v1 on v0

--- a/solution.py
+++ b/solution.py
@@ -15,16 +15,13 @@
 SIDE = 4
 MICRO = 4
 TOK = 256
-CHUNK = 128
+CHUNK = 64
 WIDTH = 1024
 SHARE = WIDTH // SHARDS
 PER_PLANE = TOK // SECTIONS
 TILE = 256
+WIDE = 512
 CHUNKS = TOK // CHUNK
-
-
-def dot_nt(a, b):
-    return lax.dot_general(a, b, (((1,), (1,)), ((), ())), preferred_element_type=F32)
 
 
 def dot_tn(a, b):
@@ -32,18 +29,21 @@
 
 
 def kernel(
-    inverse,
+    holder,
     saved,
     pooled,
     grad_top,
     w_in,
     w_out,
-    rank,
+    ids,
     out_in,
     out_out,
     out_rows,
+    out_named,
     win,
     wout,
+    win_t,
+    wout_t,
     xbuf,
     gbuf,
     nbuf,
@@ -52,6 +52,8 @@
     slope,
     dz,
     acc,
+    rank,
+    all_ids,
     sorted_rows,
     routed,
     spread,
@@ -72,6 +74,8 @@
     route_recv,
     spread_send,
     spread_recv,
+    ids_send,
+    ids_recv,
     a_send,
     a_recv,
     b_send,
@@ -137,7 +141,6 @@
         pl.semaphore_signal(
             barrier, inc=1, device_id=((sec + k) % SECTIONS, sh), device_id_type=MESH
         )
-    pl.semaphore_wait(barrier, SHARDS - 1 + SECTIONS - 1)
 
     def pool_copy(s):
         return pltpu.make_async_remote_copy(
@@ -170,33 +173,26 @@
             device_id_type=MESH,
         )
 
-    @pl.when(jnp.logical_not(first))
-    def _():
-        pool_copy(sec).start()
-
-    def clear(i, carry):
-        rows = pl.ds(pl.multiple_of(i * 64, 64), 64)
-        for mat in range(2):
-            acc[mat, rows, :] = jnp.zeros((64, WIDTH), F32)
-        return carry
-
-    lax.fori_loop(0, WIDTH // 64, clear, 0)
-
-    load_win.wait()
-
-    def micro_step(m, carry):
+    def ids_copy(k, to, came):
+        return pltpu.make_async_remote_copy(
+            src_ref=ids,
+            dst_ref=all_ids.at[came],
+            send_sem=ids_send.at[k],
+            recv_sem=ids_recv.at[k],
+            device_id=(sec, to),
+            device_id_type=MESH,
+        )
+
+    def forward(m):
         rows = micro_rows(m)
         load_x(m).wait()
 
         @pl.when(first)
         def _():
-            @pl.when(m == 0)
-            def _():
-                load_pool.wait()
-                for s in range(1, SECTIONS):
-                    pool_copy(s).wait_recv()
-
-            extra = pbuf[inverse[m]]
+            slot = 0
+            for j in range(1, MICRO):
+                slot = jnp.where(holder[j] == m, j, slot)
+            extra = pbuf[slot]
             xbuf[rows, :] = (xbuf[rows, :].astype(F32) + extra.astype(F32)).astype(BF16)
 
         for j in range(WIDTH // TILE):
@@ -206,40 +202,118 @@
             act[:, cols] = (z * sig).astype(BF16)
             slope[:, cols] = sig * (1.0 + z * (1.0 - sig))
 
-        @pl.when(m == 0)
+    def backward(c, k):
+        crows = chunk_rows(c)
+        krows = pl.ds(k * CHUNK, CHUNK)
+        for j in range(WIDTH // WIDE):
+            cols = pl.ds(j * WIDE, WIDE)
+            ga = jnp.dot(gbuf[crows, :], wout_t[:, cols], preferred_element_type=F32)
+            dz[krows, cols] = (ga * slope[krows, cols]).astype(BF16)
+        for j in range(WIDTH // WIDE):
+            cols = pl.ds(j * WIDE, WIDE)
+            back = jnp.dot(dz[krows, :], win_t[:, cols], preferred_element_type=F32)
+            nbuf[crows, cols] = (gbuf[crows, cols].astype(F32) + back).astype(BF16)
+
+    def weight_grads(m):
+        rows = micro_rows(m)
+        for i in range(WIDTH // TILE):
+            cols = pl.ds(i * TILE, TILE)
+            acc[0, cols, :] += dot_tn(xbuf[rows, cols], dz[...])
+            acc[1, cols, :] += dot_tn(act[:, cols], gbuf[rows, :])
+
+    load_win.wait()
+    for j in range(WIDTH // TILE):
+        cols = pl.ds(j * TILE, TILE)
+        win_t[:, cols] = win[cols, :].T
+
+    @pl.when(jnp.logical_not(first))
+    def _():
+        forward(0)
+
+    load_wout.wait()
+    for j in range(WIDTH // TILE):
+        cols = pl.ds(j * TILE, TILE)
+        wout_t[:, cols] = wout[cols, :].T
+
+    pl.semaphore_wait(barrier, SHARDS - 1 + SECTIONS - 1)
+
+    @pl.when(jnp.logical_not(first))
+    def _():
+        pool_copy(sec).start()
+
+    def clear(i, carry):
+        rows = pl.ds(pl.multiple_of(i * 64, 64), 64)
+        for mat in range(2):
+            acc[mat, rows, :] = jnp.zeros((64, WIDTH), F32)
+        return carry
+
+    def tell_ids(k, carry):
+        ids_copy(k, (sh + k) % SHARDS, sh).start()
+        return carry
+
+    @pl.when(first)
+    def _():
+        lax.fori_loop(0, WIDTH // 64, clear, 0)
+        lax.fori_loop(1, SHARDS, tell_ids, 0)
+        row = lax.broadcasted_iota(jnp.int32, (TOK, TOK), 0)
+        col = lax.broadcasted_iota(jnp.int32, (TOK, TOK), 1)
+        feat = ids.shape[1]
+        lane = lax.broadcasted_iota(jnp.int32, (ids.shape[2], TOK), 1)
+        lead = lax.broadcasted_iota(jnp.int32, (ids.shape[2], TOK), 0)
+        widen = jnp.where(lane >> 3 == lead, 1.0, 0.0).astype(BF16)
+        for m in range(MICRO):
+            owner = (ids[m] >> 10).astype(F32).astype(BF16)
+            wide = jnp.dot(owner, widen, preferred_element_type=F32)
+            inner = lax.broadcasted_iota(jnp.int32, (feat, TOK), 1) & 7
+            outer = lax.broadcasted_iota(jnp.int32, (feat, TOK), 0)
+            across = jnp.sum(jnp.where(inner == outer, wide, 0.0), axis=0, keepdims=True)
+            down = jnp.sum(jnp.where(row == col, across, 0.0), axis=1, keepdims=True)
+            earlier = jnp.where((down == across) & (row < col), 1.0, 0.0)
+            rank[m] = 2.0 * across + jnp.sum(earlier, axis=0, keepdims=True)
+        load_pool.wait()
+        for s in range(1, SECTIONS):
+            pool_copy(s).wait_recv()
+        forward(0)
+
+    @pl.when(last)
+    def _():
+        load_top(0).wait()
+        for k in range(CHUNKS):
+            backward(k, k)
+            relay_copy(k).start()
+
+    @pl.when(jnp.logical_not(first))
+    def _():
+        lax.fori_loop(0, WIDTH // 64, clear, 0)
+        lax.fori_loop(1, SHARDS, tell_ids, 0)
+
+    all_ids[sh] = ids[...]
+
+    def micro_step(m, carry):
+        rows = micro_rows(m)
+
+        @pl.when(jnp.logical_not(last & (m == 0)))
         def _():
-            load_wout.wait()
-
-        @pl.when(last)
-        def _():
-            load_top(m).wait()
-
-        for k in range(CHUNKS):
-            c = m * CHUNKS + k
-            crows = chunk_rows(c)
-            krows = pl.ds(k * CHUNK, CHUNK)
-
-            @pl.when(jnp.logical_not(last))
+            @pl.when(last)
             def _():
-                relay_copy(c).wait_recv()
-
-            g = gbuf[crows, :]
-            for j in range(WIDTH // TILE):
-                cols = pl.ds(j * TILE, TILE)
-                ga = dot_nt(g, wout[cols, :])
-                dz[krows, cols] = (ga * slope[krows, cols]).astype(BF16)
-            for j in range(WIDTH // TILE):
-                cols = pl.ds(j * TILE, TILE)
-                back = dot_nt(dz[krows, :], win[cols, :])
-                nbuf[crows, cols] = (gbuf[crows, cols].astype(F32) + back).astype(BF16)
-
-            @pl.when(jnp.logical_not(first))
-            def _():
-                relay_copy(c).start()
+                load_top(m).wait()
+
+            for k in range(CHUNKS):
+                c = m * CHUNKS + k
+
+                @pl.when(jnp.logical_not(last))
+                def _():
+                    relay_copy(c).wait_recv()
+
+                backward(c, k)
+
+                @pl.when(jnp.logical_not(first))
+                def _():
+                    relay_copy(c).start()
 
         @pl.when(first)
         def _():
-            target = lax.broadcasted_iota(jnp.int32, (TOK, TOK), 0)
+            target = lax.broadcasted_iota(jnp.int32, (TOK, TOK), 0).astype(F32)
             pick = jnp.where(target == rank[m], 1.0, 0.0).astype(BF16)
             ordered = jnp.dot(pick, nbuf[rows, :], preferred_element_type=F32).astype(BF16)
             sorted_rows[m] = ordered
@@ -249,13 +323,12 @@
                 :PER_PLANE, :
             ]
 
-        def weight_tile(i, inner):
-            cols = pl.ds(pl.multiple_of(i * TILE, TILE), TILE)
-            acc[0, cols, :] += dot_tn(xbuf[rows, cols], dz[...])
-            acc[1, cols, :] += dot_tn(act[:, cols], gbuf[rows, :])
-            return inner
-
-        lax.fori_loop(0, WIDTH // TILE, weight_tile, 0)
+        weight_grads(m)
+
+        @pl.when(m < MICRO - 1)
+        def _():
+            forward(m + 1)
+
         return carry
 
     lax.fori_loop(0, MICRO, micro_step, 0)
@@ -357,6 +430,35 @@
     lax.fori_loop(1, SHARDS, hand_out, 0)
     out_rows[sh] = spread[sh]
 
+    def hear_ids(k, carry):
+        ids_copy(k, (sh + k) % SHARDS, (sh + SHARDS - k) % SHARDS).wait_recv()
+        return carry
+
+    lax.fori_loop(1, SHARDS, hear_ids, 0)
+    own = sec * SHARDS + sh
+    feature = own // (SECTIONS * SHARDS // ids.shape[1])
+    heard = all_ids[:, :, feature, :].reshape(SHARDS * MICRO, ids.shape[2])
+    place = lax.broadcasted_iota(jnp.int32, heard.shape, 1) * ROWS_OWN + (heard & (ROWS_OWN - 1))
+    ours = heard >> 10 == own
+    low = jnp.min(jnp.where(ours, place, 1 << 20), axis=1, keepdims=True) & (ROWS_OWN - 1)
+    high = jnp.max(jnp.where(ours, place, -1), axis=1, keepdims=True) & (ROWS_OWN - 1)
+    at_lane = lax.broadcasted_iota(jnp.int32, (SHARDS * MICRO, 128), 1)
+    parts = jnp.where(
+        at_lane == 0,
+        low >> 5,
+        jnp.where(at_lane == 1, low & 31, jnp.where(at_lane == 2, high >> 5, high & 31)),
+    )
+    half = lax.broadcasted_iota(jnp.int32, (TOK, SHARDS * MICRO), 0) >> 1
+    twice = jnp.where(
+        half == lax.broadcasted_iota(jnp.int32, (TOK, SHARDS * MICRO), 1), 1.0, 0.0
+    ).astype(BF16)
+    both = jnp.dot(twice, parts.astype(F32).astype(BF16), preferred_element_type=F32)
+    odd = lax.broadcasted_iota(jnp.int32, (TOK, 1), 0) & 1
+    row_of = jnp.where(
+        odd == 0, both[:, 0:1] * 32.0 + both[:, 1:2], both[:, 2:3] * 32.0 + both[:, 3:4]
+    )
+    out_named[...] = jnp.broadcast_to(row_of.astype(jnp.int32), (TOK, 128))
+
     for d in range(1, SIDE):
         for mat in range(2):
             b_copy(mat, d).wait_recv()
@@ -409,6 +511,12 @@
         return carry
 
     lax.fori_loop(1, SHARDS, spread_left, 0)
+
+    def ids_left(k, carry):
+        ids_copy(k, (sh + k) % SHARDS, sh).wait_send()
+        return carry
+
+    lax.fori_loop(1, SHARDS, ids_left, 0)
     for mat in range(2):
         for t in range(SIDE):
             a_copy(mat, t).wait_send()
@@ -417,7 +525,7 @@
             c_copy(mat, d).wait_send()
 
 
-def relay(inverse, saved, pooled, grad_top, w_in, w_out, rank):
+def relay(holder, saved, pooled, grad_top, w_in, w_out, ids):
     vmem = pl.BlockSpec(memory_space=pltpu.VMEM)
     anywhere = pl.BlockSpec(memory_space=pl.ANY)
     dma = pltpu.SemaphoreType.DMA
@@ -428,10 +536,13 @@
             jax.ShapeDtypeStruct((SHARE, WIDTH), F32),
             jax.ShapeDtypeStruct((SHARE, WIDTH), F32),
             jax.ShapeDtypeStruct((SHARDS, 2 * MICRO, WIDTH), BF16),
+            jax.ShapeDtypeStruct((TOK, 128), jnp.int32),
         ),
         in_specs=[pl.BlockSpec(memory_space=pltpu.SMEM)] + [anywhere] * 5 + [vmem],
-        out_specs=(vmem, vmem, vmem),
+        out_specs=(vmem, vmem, vmem, vmem),
         scratch_shapes=[
+            pltpu.VMEM((WIDTH, WIDTH), BF16),
+            pltpu.VMEM((WIDTH, WIDTH), BF16),
             pltpu.VMEM((WIDTH, WIDTH), BF16),
             pltpu.VMEM((WIDTH, WIDTH), BF16),
             pltpu.VMEM((tokens, WIDTH), BF16),
@@ -442,6 +553,8 @@
             pltpu.VMEM((TOK, WIDTH), F32),
             pltpu.VMEM((TOK, WIDTH), BF16),
             pltpu.VMEM((2, WIDTH, WIDTH), F32),
+            pltpu.VMEM((MICRO, 1, TOK), F32),
+            pltpu.VMEM((SHARDS,) + ids.shape, jnp.int32),
             pltpu.VMEM((MICRO, TOK, WIDTH), BF16),
             pltpu.VMEM((TOK, WIDTH), BF16),
             pltpu.VMEM((SHARDS, 2 * MICRO, WIDTH), BF16),
@@ -462,6 +575,8 @@
             dma((MICRO,)),
             dma((SHARDS,)),
             dma((SHARDS,)),
+            dma((SHARDS,)),
+            dma((SHARDS,)),
             dma((2, SIDE)),
             dma((2, SIDE)),
             dma((2, SIDE - 1)),
@@ -476,41 +591,59 @@
             flops=10 * tokens * WIDTH * WIDTH, bytes_accessed=9 * 2**20, transcendentals=tokens * WIDTH
         ),
         name="relay",
-    )(inverse, saved, pooled, grad_top, w_in, w_out, rank)
+    )(holder, saved, pooled, grad_top, w_in, w_out, ids)
+
+
+def table_kernel(named, rows, grad_in, grad_out, table, out_in, out_out):
+    block = pl.program_id(0)
+    lane = lax.broadcasted_iota(jnp.int32, (TOK, TILE), 1) + block * TILE
+    hit = jnp.where(lane == named[:, 0:1], 1.0, 0.0).astype(BF16)
+    table[...] = dot_tn(hit, rows[...])
+
+    @pl.when(block == 0)
+    def _():
+        out_in[...] = grad_in[...]
+        out_out[...] = grad_out[...]
+
+
+def owner_sums(named, rows, grad_in, grad_out):
+    def whole(array):
+        return pl.BlockSpec(array.shape, lambda b: (0, 0))
+
+    return pl.pallas_call(
+        table_kernel,
+        grid=(ROWS_OWN // TILE,),
+        out_shape=(
+            jax.ShapeDtypeStruct((ROWS_OWN, WIDTH), F32),
+            jax.ShapeDtypeStruct(grad_in.shape, F32),
+            jax.ShapeDtypeStruct(grad_out.shape, F32),
+        ),
+        in_specs=[whole(named), whole(rows), whole(grad_in), whole(grad_out)],
+        out_specs=(
+            pl.BlockSpec((TILE, WIDTH), lambda b: (b, 0)),
+            whole(grad_in),
+            whole(grad_out),
+        ),
+        cost_estimate=pl.CostEstimate(
+            flops=2 * ROWS_OWN * TOK * WIDTH, bytes_accessed=5 * 2**20, transcendentals=0
+        ),
+        name="owner_sums",
+    )(named, rows, grad_in, grad_out)
 
 
 def local(saved, pooled, grad_top, w_in, w_out, feature_ids, holder_order):
-    section_id = lax.axis_index("section")
-    shard_id = lax.axis_index("shard")
     tokens = MICRO * TOK
-    micro_range = jnp.arange(MICRO, dtype=jnp.int32)
-    inverse = jnp.sum(
-        jnp.where(holder_order[None, :] == micro_range[:, None], micro_range[None, :], 0), axis=1
-    )
-    ids = feature_ids.reshape(MICRO, TOK)
-    owner = ids // ROWS_OWN
-    position = jnp.arange(TOK, dtype=jnp.int32)
-    earlier = (owner[:, :, None] == owner[:, None, :]) & (position[None, :] < position[:, None])
-    rank = 2 * owner + jnp.sum(earlier.astype(jnp.int32), axis=2)
-    out_in, out_out, rows = relay(
-        inverse,
+    out_in, out_out, rows, named = relay(
+        holder_order,
         saved.reshape(tokens, WIDTH),
         pooled.reshape(TOK, WIDTH),
         grad_top.reshape(tokens, WIDTH),
         w_in[0],
         w_out[0],
-        rank.reshape(MICRO, 1, TOK),
+        jnp.transpose(feature_ids, (0, 2, 1)),
     )
-    all_ids = lax.all_gather(ids, "shard", axis=0)
-    own = section_id * SHARDS + shard_id
-    key = position * ROWS_OWN + all_ids % ROWS_OWN
-    named = all_ids // ROWS_OWN == own
-    low = jnp.min(jnp.where(named, key, TOK * ROWS_OWN), axis=2)
-    high = jnp.max(jnp.where(named, key, -1), axis=2)
-    row_of = (jnp.stack([low, high], axis=2) % ROWS_OWN).reshape(-1)
-    one_hot = (jnp.arange(ROWS_OWN, dtype=jnp.int32)[:, None] == row_of[None, :]).astype(BF16)
-    table_grad = jnp.dot(one_hot, rows.reshape(-1, WIDTH), preferred_element_type=F32)
-    return (out_in[None], out_out[None], table_grad)
+    table_grad, grad_in, grad_out = owner_sums(named, rows.reshape(TOK, WIDTH), out_in, out_out)
+    return (grad_in[None], grad_out[None], table_grad)
 
 
 def solution(mesh):

time: 140 us -> 104 us (0.74)
  blocking collectives: 26.2 us -> 0 us
  matrix products: 3.81 us -> 0 us
  other arithmetic: 3.53 us -> 0 us
  local copies, waits for them, and re-layouts: 2.83 us -> 0 us
    all_gather x1 -> x0, blocking collectives: 26.2 us -> none  [local(): all_ids = lax.all_gather(ids, 'shard', axis=0)]
    pallas_call x1, Pallas kernels: 103 us -> 98.5 us  [relay(): pl.pallas_call(kernel, out_shape=(jax.ShapeDtypeStruct((SHARE, WIDTH), F3...]
    pallas_call x0 -> x1, Pallas kernels: none -> 4.44 us  [owner_sums(): pl.pallas_call(table_kernel, grid=(ROWS_OWN // TILE,), out_shape=(jax.Sha...]
    dot_general x1 -> x0, matrix products: 3.81 us -> none  [local(): jnp.dot(one_hot, rows.reshape(-1, WIDTH), preferred_element_type=F32)]
    unnamed x7 -> x0, local copies, waits for them, and re-layouts: 2.11 us -> none
    reduce_sum x2 -> x0, other arithmetic: 1.68 us -> none  [the longest x1 1.28 us: local(): jnp.sum(jnp.where(holder_order[None, :] == micro_range[:, None], micro_ra...]
where the time goes in v1:
time: 104 us
  Pallas kernels  103 us (99%)
    pallas_call x1, Pallas kernels, relay(): pl.pallas_call(kernel, out_shape=(jax.ShapeDtypeStruct((SHARE, WIDTH), F3...  98.5 us
    pallas_call x1, Pallas kernels, owner_sums(): pl.pallas_call(table_kernel, grid=(ROWS_OWN // TILE,), out_shape=(jax.Sha...  4.44 us

profile of v1, /device:TPU:1, one launch (start us, length us, event | category | flops | bytes accessed | tf_op | source)
XLA Modules:
  0.0 103.6 jit_solution(6523226796283412483)
XLA Ops:
  0.6 98.5 %relay.1 = (f32[32,1024]{1,0:T(8,128)}, f32[32,1024]{1,0:T(8,128)}, bf16[32,8,1024]{2,1,0:T(8,128)(2,1)}, s32[256,128]{1,0:T(8,128)}) custom-call(s32[4]{0:T(128)} %holder.1, bf16[1024,1024]{1,0:T(8,128)(2,1)} %bitcast.9, bf16[256,1024]{1,0:T(8,128)(2,1)} %bitcast.13, bf16[1024,1024]{1,0:T(8,128)(2,1)} %bitcast.10, bf16[1024,1024]{1,0:T(8,128)(2,1)} %bitcast.11, ...), custom_call_target="tpu_custom_call" | custom-call | flops 10737418240 | bytes 9437184 | tf_op jit(solution)/shard_map/relay/pallas_call | solution.py:533
  99.1 4.4 %owner_sums.1 = (f32[1024,1024]{1,0:T(8,128)}, f32[32,1024]{1,0:T(8,128)}, f32[32,1024]{1,0:T(8,128)}) custom-call(s32[256,128]{1,0:T(8,128)} %get-tuple-element.10.named, bf16[256,1024]{1,0:T(8,128)(2,1)} %bitcast.15, f32[32,1024]{1,0:T(8,128)} %get-tuple-element.12.grad_in, f32[32,1024]{1,0:T(8,128)} %get-tuple-element.13.grad_out), custom_call_target="tpu_custom_call" | custom-call | flops 536870912 | bytes 5242880 | tf_op jit(solution)/shard_map/owner_sums/pallas_call | solution.py:613

commit v2 on v1

--- a/solution.py
+++ b/solution.py
@@ -16,12 +16,18 @@
 MICRO = 4
 TOK = 256
 CHUNK = 64
+LATE = 32
 WIDTH = 1024
 SHARE = WIDTH // SHARDS
 PER_PLANE = TOK // SECTIONS
 TILE = 256
 WIDE = 512
 CHUNKS = TOK // CHUNK
+EARLY = (MICRO - 1) * CHUNKS
+LATES = TOK // LATE
+PIECES = EARLY + LATES
+HALF = WIDTH // 2
+BLOCK = 2 * SHARE
 
 
 def dot_tn(a, b):
@@ -57,11 +63,13 @@
     sorted_rows,
     routed,
     spread,
-    send_a,
-    recv_a,
-    send_b,
-    recv_b,
-    own_b,
+    peer_l,
+    peer_r,
+    send_x,
+    recv_x,
+    send_y,
+    recv_y,
+    own_c,
     send_c,
     recv_c,
     load_sem,
@@ -76,10 +84,14 @@
     spread_recv,
     ids_send,
     ids_recv,
-    a_send,
-    a_recv,
-    b_send,
-    b_recv,
+    l_send,
+    l_recv,
+    r_send,
+    r_recv,
+    x_send,
+    x_recv,
+    y_send,
+    y_recv,
     c_send,
     c_recv,
 ):
@@ -97,8 +109,9 @@
     def micro_rows(m):
         return pl.ds(pl.multiple_of(m * TOK, TOK), TOK)
 
-    def chunk_rows(c):
-        return pl.ds(pl.multiple_of(c * CHUNK, CHUNK), CHUNK)
+    def chunk_rows(c, size):
+        start = c * CHUNK if size == CHUNK else EARLY * CHUNK + (c - EARLY) * LATE
+        return pl.ds(pl.multiple_of(start, size), size)
 
     def load_x(m):
         rows = micro_rows(m)
@@ -152,8 +165,8 @@
             device_id_type=MESH,
         )
 
-    def relay_copy(c):
-        rows = chunk_rows(c)
+    def relay_copy(c, size):
+        rows = chunk_rows(c, size)
         return pltpu.make_async_remote_copy(
             src_ref=nbuf.at[rows],
             dst_ref=gbuf.at[rows],
@@ -183,6 +196,46 @@
             device_id_type=MESH,
         )
 
+    def left_copy(m, source):
+        rows = micro_rows(m)
+        return pltpu.make_async_remote_copy(
+            src_ref=source.at[rows],
+            dst_ref=peer_l.at[rows],
+            send_sem=l_send.at[m],
+            recv_sem=l_recv.at[m],
+            device_id=at(py, px, 1 - core),
+            device_id_type=MESH,
+        )
+
+    def right_copy(n, source, start, size):
+        rows = pl.ds(pl.multiple_of(start, 64), size)
+        return pltpu.make_async_remote_copy(
+            src_ref=source.at[rows],
+            dst_ref=peer_r.at[rows],
+            send_sem=r_send.at[n],
+            recv_sem=r_recv.at[n],
+            device_id=at(py, px, 1 - core),
+            device_id_type=MESH,
+        )
+
+    def send_left(m):
+        @pl.when(core == 0)
+        def _():
+            left_copy(m, act).start()
+
+        @pl.when(core == 1)
+        def _():
+            left_copy(m, xbuf).start()
+
+    def send_right(n, start, size):
+        @pl.when(core == 0)
+        def _():
+            right_copy(n, gbuf, start, size).start()
+
+        @pl.when(core == 1)
+        def _():
+            right_copy(n, dz, start, size).start()
+
     def forward(m):
         rows = micro_rows(m)
         load_x(m).wait()
@@ -199,27 +252,38 @@
             cols = pl.ds(j * TILE, TILE)
             z = jnp.dot(xbuf[rows, :], win[:, cols], preferred_element_type=F32)
             sig = jax.nn.sigmoid(z)
-            act[:, cols] = (z * sig).astype(BF16)
+            act[rows, cols] = (z * sig).astype(BF16)
             slope[:, cols] = sig * (1.0 + z * (1.0 - sig))
 
-    def backward(c, k):
-        crows = chunk_rows(c)
-        krows = pl.ds(k * CHUNK, CHUNK)
+    def backward(c, k, size):
+        crows = chunk_rows(c, size)
+        krows = pl.ds(k * size, size)
         for j in range(WIDTH // WIDE):
             cols = pl.ds(j * WIDE, WIDE)
             ga = jnp.dot(gbuf[crows, :], wout_t[:, cols], preferred_element_type=F32)
-            dz[krows, cols] = (ga * slope[krows, cols]).astype(BF16)
+            dz[crows, cols] = (ga * slope[krows, cols]).astype(BF16)
         for j in range(WIDTH // WIDE):
             cols = pl.ds(j * WIDE, WIDE)
-            back = jnp.dot(dz[krows, :], win_t[:, cols], preferred_element_type=F32)
+            back = jnp.dot(dz[crows, :], win_t[:, cols], preferred_element_type=F32)
             nbuf[crows, cols] = (gbuf[crows, cols].astype(F32) + back).astype(BF16)
 
+    def own_grads(m, and_peer):
+        rows = micro_rows(m)
+        for kind, left, right in ((0, xbuf, dz), (1, act, gbuf)):
+
+            @pl.when(core == kind)
+            def _(left=left, right=right):
+                for i in range(WIDTH // TILE):
+                    cols = pl.ds(i * TILE, TILE)
+                    total = acc[cols, :] + dot_tn(left[rows, cols], right[rows, :])
+                    if and_peer:
+                        total = total + dot_tn(peer_l[rows, cols], peer_r[rows, :])
+                    acc[cols, :] = total
+
     def weight_grads(m):
-        rows = micro_rows(m)
-        for i in range(WIDTH // TILE):
-            cols = pl.ds(i * TILE, TILE)
-            acc[0, cols, :] += dot_tn(xbuf[rows, cols], dz[...])
-            acc[1, cols, :] += dot_tn(act[:, cols], gbuf[rows, :])
+        left_copy(m, act).wait_recv()
+        right_copy(m, dz, m * TOK, TOK).wait_recv()
+        own_grads(m, True)
 
     load_win.wait()
     for j in range(WIDTH // TILE):
@@ -243,8 +307,7 @@
 
     def clear(i, carry):
         rows = pl.ds(pl.multiple_of(i * 64, 64), 64)
-        for mat in range(2):
-            acc[mat, rows, :] = jnp.zeros((64, WIDTH), F32)
+        acc[rows, :] = jnp.zeros((64, WIDTH), F32)
         return carry
 
     def tell_ids(k, carry):
@@ -279,8 +342,8 @@
     def _():
         load_top(0).wait()
         for k in range(CHUNKS):
-            backward(k, k)
-            relay_copy(k).start()
+            backward(k, k, CHUNK)
+            relay_copy(k, CHUNK).start()
 
     @pl.when(jnp.logical_not(first))
     def _():
@@ -288,28 +351,21 @@
         lax.fori_loop(1, SHARDS, tell_ids, 0)
 
     all_ids[sh] = ids[...]
-
-    def micro_step(m, carry):
+    send_left(0)
+
+    def step(c, k, size):
+        @pl.when(jnp.logical_not(last))
+        def _():
+            relay_copy(c, size).wait_recv()
+
+        backward(c, k, size)
+
+        @pl.when(jnp.logical_not(first))
+        def _():
+            relay_copy(c, size).start()
+
+    def route(m):
         rows = micro_rows(m)
-
-        @pl.when(jnp.logical_not(last & (m == 0)))
-        def _():
-            @pl.when(last)
-            def _():
-                load_top(m).wait()
-
-            for k in range(CHUNKS):
-                c = m * CHUNKS + k
-
-                @pl.when(jnp.logical_not(last))
-                def _():
-                    relay_copy(c).wait_recv()
-
-                backward(c, k)
-
-                @pl.when(jnp.logical_not(first))
-                def _():
-                    relay_copy(c).start()
 
         @pl.when(first)
         def _():
@@ -323,83 +379,100 @@
                 :PER_PLANE, :
             ]
 
-        weight_grads(m)
-
-        @pl.when(m < MICRO - 1)
-        def _():
-            forward(m + 1)
-
-        return carry
-
-    lax.fori_loop(0, MICRO, micro_step, 0)
-
-    def mine(mat):
-        return px if mat == 0 else py
-
-    def acc_rows(mat, t, o, c):
-        block = (o * SIDE + t) if mat == 0 else (t * SIDE + o)
-        return pl.ds(pl.multiple_of(block * 2 * SHARE + c * SHARE, SHARE), SHARE)
-
-    def a_copy(mat, t):
-        return pltpu.make_async_remote_copy(
-            src_ref=send_a.at[mat, t],
-            dst_ref=recv_a.at[mat, t],
-            send_sem=a_send.at[mat, t],
-            recv_sem=a_recv.at[mat, t],
-            device_id=at(py, px, 1 - core),
-            device_id_type=MESH,
-        )
-
-    def b_copy(mat, d):
-        t = (mine(mat) + d) % SIDE
-        return pltpu.make_async_remote_copy(
-            src_ref=send_b.at[mat, d - 1],
-            dst_ref=recv_b.at[mat, d - 1],
-            send_sem=b_send.at[mat, d - 1],
-            recv_sem=b_recv.at[mat, d - 1],
-            device_id=at(py, t, core) if mat == 0 else at(t, px, core),
-            device_id_type=MESH,
-        )
-
-    def c_copy(mat, d):
-        t = (mine(1 - mat) + d) % SIDE
-        return pltpu.make_async_remote_copy(
-            src_ref=send_c.at[mat, d - 1],
-            dst_ref=recv_c.at[mat, d - 1],
-            send_sem=c_send.at[mat, d - 1],
-            recv_sem=c_recv.at[mat, d - 1],
-            device_id=at(t, px, core) if mat == 0 else at(py, t, core),
+    def micro_step(m, carry):
+        @pl.when(jnp.logical_not(last & (m == 0)))
+        def _():
+            @pl.when(last)
+            def _():
+                load_top(m).wait()
+
+            for k in range(CHUNKS):
+                step(m * CHUNKS + k, k, CHUNK)
+                if k == 0:
+
+                    @pl.when(m > 0)
+                    def _():
+                        weight_grads(m - 1)
+
+        send_right(m, m * TOK, TOK)
+        route(m)
+        forward(m + 1)
+        send_left(m + 1)
+        return carry
+
+    lax.fori_loop(0, MICRO - 1, micro_step, 0)
+
+    final = MICRO - 1
+    tail = TOK - 2 * LATE
+
+    @pl.when(last)
+    def _():
+        load_top(final).wait()
+
+    for k in range(LATES):
+        step(EARLY + k, k, LATE)
+        if k == 0:
+            weight_grads(final - 1)
+        if k == LATES - 3:
+            send_right(final, final * TOK, tail)
+    send_right(final + 1, final * TOK + tail, TOK - tail)
+    route(final)
+    own_grads(final, False)
+
+    def block_rows(y, x):
+        return pl.ds(pl.multiple_of((y * SIDE + x) * BLOCK, BLOCK), BLOCK)
+
+    left_half = pl.ds(0, HALF)
+    right_half = pl.ds(HALF, HALF)
+
+    def x_copy(d, y):
+        to = (px + d) % SIDE
+        return pltpu.make_async_remote_copy(
+            src_ref=send_x.at[y, pl.ds(pl.multiple_of(to * BLOCK, BLOCK), BLOCK)],
+            dst_ref=recv_x.at[d - 1, y],
+            send_sem=x_send.at[d - 1, y],
+            recv_sem=x_recv.at[d - 1, y],
+            device_id=at(py, to, core),
+            device_id_type=MESH,
+        )
+
+    def y_copy(d):
+        return pltpu.make_async_remote_copy(
+            src_ref=send_y.at[d - 1],
+            dst_ref=recv_y.at[d - 1],
+            send_sem=y_send.at[d - 1],
+            recv_sem=y_recv.at[d - 1],
+            device_id=at((py + d) % SIDE, px, core),
+            device_id_type=MESH,
+        )
+
+    def c_copy(h, e, c, kind):
+        there = (py + e) % SIDE if h == 0 else (px + e) % SIDE
+        return pltpu.make_async_remote_copy(
+            src_ref=send_c.at[h, e, c],
+            dst_ref=recv_c.at[kind, h, e],
+            send_sem=c_send.at[h, e, c],
+            recv_sem=c_recv.at[kind, h, e],
+            device_id=at(there, px, c) if h == 0 else at(py, there, c),
             device_id_type=MESH,
         )
 
     order = (2, 1, 3, 0)
+    frows = micro_rows(final)
+    left_copy(final, act).wait_recv()
+    right_copy(final, dz, final * TOK, tail).wait_recv()
+    right_copy(final + 1, dz, final * TOK + tail, TOK - tail).wait_recv()
     for d in order:
-        for mat in range(2):
-            t = (mine(mat) + d) % SIDE
-
-            def fill_a(o, carry, mat=mat, t=t):
-                send_a[mat, t, o] = acc[mat, acc_rows(mat, t, o, 1 - core), :].astype(BF16)
-                return carry
-
-            lax.fori_loop(0, SIDE, fill_a, 0)
-            a_copy(mat, t).start()
-
-    for d in order:
-        for mat in range(2):
-            t = (mine(mat) + d) % SIDE
-            a_copy(mat, t).wait_recv()
-
-            def add_a(o, carry, mat=mat, t=t, d=d):
-                both = acc[mat, acc_rows(mat, t, o, core), :] + recv_a[mat, t, o].astype(F32)
-                if d == 0:
-                    own_b[mat, o] = both
-                else:
-                    send_b[mat, d - 1, o] = both.astype(BF16)
-                return carry
-
-            lax.fori_loop(0, SIDE, add_a, 0)
-            if d != 0:
-                b_copy(mat, d).start()
+        y = (py + d) % SIDE
+        cols = pl.ds(pl.multiple_of(y * TILE, TILE), TILE)
+        total = acc[cols, :] + dot_tn(peer_l[frows, cols], peer_r[frows, :])
+        acc[cols, :] = total
+        send_x[y] = total[:, :HALF].astype(BF16)
+        for dx in (2, 1, 3):
+            x_copy(dx, y).start()
+        if d != 0:
+            send_y[d - 1] = total[:, HALF:].astype(BF16)
+            y_copy(d).start()
 
     @pl.when(jnp.logical_not(first))
     def _():
@@ -460,29 +533,50 @@
     out_named[...] = jnp.broadcast_to(row_of.astype(jnp.int32), (TOK, 128))
 
     for d in range(1, SIDE):
-        for mat in range(2):
-            b_copy(mat, d).wait_recv()
-    for mat in range(2):
-
-        def add_b(o, carry, mat=mat):
-            total = own_b[mat, o]
-            for d in range(1, SIDE):
-                total = total + recv_b[mat, d - 1, o].astype(F32)
-            own_b[mat, o] = total
-            return carry
-
-        lax.fori_loop(0, SIDE, add_b, 0)
-        for d in (2, 1, 3):
-            t = (mine(1 - mat) + d) % SIDE
-            send_c[mat, d - 1] = own_b[mat, t].astype(BF16)
-            c_copy(mat, d).start()
-
-    for mat, out in ((0, out_in), (1, out_out)):
-        total = own_b[mat, mine(1 - mat)]
+        y_copy(d).wait_recv()
+    for e in order:
+        y = (py + e) % SIDE
         for d in range(1, SIDE):
-            c_copy(mat, d).wait_recv()
-            total = total + recv_c[mat, d - 1].astype(F32)
-        out[...] = total
+            x_copy(d, y).wait_recv()
+        x = (px + e) % SIDE
+        total = acc[block_rows(y, px), left_half]
+        other = acc[block_rows(py, x), right_half]
+        for d in range(1, SIDE):
+            total = total + recv_x[d - 1, y].astype(F32)
+            xrows = pl.ds(pl.multiple_of(x * BLOCK, BLOCK), BLOCK)
+            other = other + recv_y[d - 1, xrows, :].astype(F32)
+        for h, part in ((0, total), (1, other)):
+            for c in range(2):
+                send_c[h, e, c] = part[c * SHARE : (c + 1) * SHARE, :].astype(BF16)
+                if e == 0:
+
+                    @pl.when(core == c)
+                    def _(h=h, c=c, part=part):
+                        own_c[h] = part[c * SHARE : (c + 1) * SHARE, :]
+
+                    @pl.when(core != c)
+                    def _(h=h, c=c):
+                        c_copy(h, 0, c, core).start()
+                else:
+                    c_copy(h, e, c, core).start()
+
+    for kind, out in ((0, out_in), (1, out_out)):
+        for h, cols in ((0, left_half), (1, right_half)):
+
+            @pl.when(core == kind)
+            def _(h=h, out=out, cols=cols):
+                out[:, cols] = own_c[h]
+
+            @pl.when(core != kind)
+            def _(h=h, out=out, cols=cols, kind=kind):
+                c_copy(h, 0, 1 - kind, kind).wait_recv()
+                out[:, cols] = recv_c[kind, h, 0].astype(F32)
+
+            total = out[:, cols]
+            for e in range(1, SIDE):
+                c_copy(h, e, 0, kind).wait_recv()
+                total = total + recv_c[kind, h, e].astype(F32)
+            out[:, cols] = total
 
     def collect(k, carry):
         spread_copy(k, (sh + k) % SHARDS, (sh + SHARDS - k) % SHARDS).wait_recv()
@@ -495,10 +589,16 @@
         pool_copy(sec).wait_send()
 
         def left(c, carry):
-            relay_copy(c).wait_send()
+            relay_copy(c, CHUNK).wait_send()
             return carry
 
-        lax.fori_loop(0, MICRO * CHUNKS, left, 0)
+        lax.fori_loop(0, EARLY, left, 0)
+
+        def left_late(c, carry):
+            relay_copy(c, LATE).wait_send()
+            return carry
+
+        lax.fori_loop(EARLY, PIECES, left_late, 0)
 
     @pl.when(first)
     def _():
@@ -517,12 +617,21 @@
         return carry
 
     lax.fori_loop(1, SHARDS, ids_left, 0)
-    for mat in range(2):
-        for t in range(SIDE):
-            a_copy(mat, t).wait_send()
-        for d in range(1, SIDE):
-            b_copy(mat, d).wait_send()
-            c_copy(mat, d).wait_send()
+    for m in range(MICRO):
+        left_copy(m, act).wait_send()
+    for m in range(final):
+        right_copy(m, dz, m * TOK, TOK).wait_send()
+    right_copy(final, dz, final * TOK, tail).wait_send()
+    right_copy(final + 1, dz, final * TOK + tail, TOK - tail).wait_send()
+    for d in range(1, SIDE):
+        y_copy(d).wait_send()
+        for y in range(SIDE):
+            x_copy(d, y).wait_send()
+        for h in range(2):
+            for c in range(2):
+                c_copy(h, d, c, core).wait_send()
+    for h in range(2):
+        c_copy(h, 0, 1 - core, core).wait_send()
 
 
 def relay(holder, saved, pooled, grad_top, w_in, w_out, ids):
@@ -549,40 +658,46 @@
             pltpu.VMEM((tokens, WIDTH), BF16),
             pltpu.VMEM((tokens, WIDTH), BF16),
             pltpu.VMEM((SECTIONS, TOK, WIDTH), BF16),
-            pltpu.VMEM((TOK, WIDTH), BF16),
+            pltpu.VMEM((tokens, WIDTH), BF16),
             pltpu.VMEM((TOK, WIDTH), F32),
-            pltpu.VMEM((TOK, WIDTH), BF16),
-            pltpu.VMEM((2, WIDTH, WIDTH), F32),
+            pltpu.VMEM((tokens, WIDTH), BF16),
+            pltpu.VMEM((WIDTH, WIDTH), F32),
             pltpu.VMEM((MICRO, 1, TOK), F32),
             pltpu.VMEM((SHARDS,) + ids.shape, jnp.int32),
             pltpu.VMEM((MICRO, TOK, WIDTH), BF16),
             pltpu.VMEM((TOK, WIDTH), BF16),
             pltpu.VMEM((SHARDS, 2 * MICRO, WIDTH), BF16),
-            pltpu.VMEM((2, SIDE, SIDE, SHARE, WIDTH), BF16),
-            pltpu.VMEM((2, SIDE, SIDE, SHARE, WIDTH), BF16),
-            pltpu.VMEM((2, SIDE - 1, SIDE, SHARE, WIDTH), BF16),
-            pltpu.VMEM((2, SIDE - 1, SIDE, SHARE, WIDTH), BF16),
-            pltpu.VMEM((2, SIDE, SHARE, WIDTH), F32),
-            pltpu.VMEM((2, SIDE - 1, SHARE, WIDTH), BF16),
-            pltpu.VMEM((2, SIDE - 1, SHARE, WIDTH), BF16),
+            pltpu.VMEM((tokens, WIDTH), BF16),
+            pltpu.VMEM((tokens, WIDTH), BF16),
+            pltpu.VMEM((SIDE, SIDE * BLOCK, HALF), BF16),
+            pltpu.VMEM((SIDE - 1, SIDE, BLOCK, HALF), BF16),
+            pltpu.VMEM((SIDE - 1, SIDE * BLOCK, HALF), BF16),
+            pltpu.VMEM((SIDE - 1, SIDE * BLOCK, HALF), BF16),
+            pltpu.VMEM((2, SHARE, HALF), F32),
+            pltpu.VMEM((2, SIDE, 2, SHARE, HALF), BF16),
+            pltpu.VMEM((2, 2, SIDE, SHARE, HALF), BF16),
             dma((3 + MICRO,)),
             dma((MICRO,)),
             dma,
             dma((SECTIONS,)),
-            dma((MICRO * CHUNKS,)),
-            dma((MICRO * CHUNKS,)),
+            dma((PIECES,)),
+            dma((PIECES,)),
             dma((MICRO, SECTIONS)),
             dma((MICRO,)),
             dma((SHARDS,)),
             dma((SHARDS,)),
             dma((SHARDS,)),
             dma((SHARDS,)),
-            dma((2, SIDE)),
-            dma((2, SIDE)),
-            dma((2, SIDE - 1)),
-            dma((2, SIDE - 1)),
-            dma((2, SIDE - 1)),
-            dma((2, SIDE - 1)),
+            dma((MICRO,)),
+            dma((MICRO,)),
+            dma((MICRO + 1,)),
+            dma((MICRO + 1,)),
+            dma((SIDE - 1, SIDE)),
+            dma((SIDE - 1, SIDE)),
+            dma((SIDE - 1,)),
+            dma((SIDE - 1,)),
+            dma((2, SIDE, 2)),
+            dma((2, 2, SIDE)),
         ],
         compiler_params=pltpu.CompilerParams(
             collective_id=0, has_side_effects=True, vmem_limit_bytes=56 * 1024 * 1024

time: 104 us -> 103 us (level)
  no operation moved by 1% of the time
where the time goes in v2:
time: 103 us
  Pallas kernels  102 us (99%)
    pallas_call x1, Pallas kernels, relay(): pl.pallas_call(kernel, out_shape=(jax.ShapeDtypeStruct((SHARE, WIDTH), F3...  97.8 us
    pallas_call x1, Pallas kernels, owner_sums(): pl.pallas_call(table_kernel, grid=(ROWS_OWN // TILE,), out_shape=(jax.Sha...  4.44 us

profile of v2, /device:TPU:1, one launch (start us, length us, event | category | flops | bytes accessed | tf_op | source)
XLA Modules:
  0.0 102.9 jit_solution(15429246600851884008)
XLA Ops:
  0.6 97.8 %relay.1 = (f32[32,1024]{1,0:T(8,128)}, f32[32,1024]{1,0:T(8,128)}, bf16[32,8,1024]{2,1,0:T(8,128)(2,1)}, s32[256,128]{1,0:T(8,128)}) custom-call(s32[4]{0:T(128)} %holder.1, bf16[1024,1024]{1,0:T(8,128)(2,1)} %bitcast.9, bf16[256,1024]{1,0:T(8,128)(2,1)} %bitcast.13, bf16[1024,1024]{1,0:T(8,128)(2,1)} %bitcast.10, bf16[1024,1024]{1,0:T(8,128)(2,1)} %bitcast.11, ...), custom_call_target="tpu_custom_call" | custom-call | flops 10737418240 | bytes 9437184 | tf_op jit(solution)/shard_map/relay/pallas_call | solution.py:642
  98.4 4.4 %owner_sums.1 = (f32[1024,1024]{1,0:T(8,128)}, f32[32,1024]{1,0:T(8,128)}, f32[32,1024]{1,0:T(8,128)}) custom-call(s32[256,128]{1,0:T(8,128)} %get-tuple-element.10.named, bf16[256,1024]{1,0:T(8,128)(2,1)} %bitcast.15, f32[32,1024]{1,0:T(8,128)} %get-tuple-element.12.grad_in, f32[32,1024]{1,0:T(8,128)} %get-tuple-element.13.grad_out), custom_call_target="tpu_custom_call" | custom-call | flops 536870912 | bytes 5242880 | tf_op jit(solution)/shard_map/owner_sums/pallas_call | solution.py:728

commit v3 on v2

--- a/solution.py
+++ b/solution.py
@@ -23,9 +23,9 @@
 TILE = 256
 WIDE = 512
 CHUNKS = TOK // CHUNK
-EARLY = (MICRO - 1) * CHUNKS
-LATES = TOK // LATE
-PIECES = EARLY + LATES
+EARLY = MICRO * CHUNKS - 1
+PIECES = EARLY + CHUNK // LATE
+SOON = (MICRO - 1) * PER_PLANE
 HALF = WIDTH // 2
 BLOCK = 2 * SHARE
 
@@ -62,7 +62,11 @@
     all_ids,
     sorted_rows,
     routed,
-    spread,
+    soon,
+    got_soon,
+    late,
+    got_late,
+    flat,
     peer_l,
     peer_r,
     send_x,
@@ -80,8 +84,11 @@
     relay_recv,
     route_send,
     route_recv,
-    spread_send,
-    spread_recv,
+    soon_send,
+    soon_recv,
+    late_send,
+    late_recv,
+    ready,
     ids_send,
     ids_recv,
     l_send,
@@ -143,17 +150,32 @@
 
     barrier = pltpu.get_barrier_semaphore()
 
-    def greet(k, carry):
-        pl.semaphore_signal(
-            barrier, inc=1, device_id=(sec, (sh + k) % SHARDS), device_id_type=MESH
-        )
-        return carry
-
-    lax.fori_loop(1, SHARDS, greet, 0)
+    def greet(y, x, c):
+        pl.semaphore_signal(barrier, inc=1, device_id=at(y, x, c), device_id_type=MESH)
+
     for k in range(1, SECTIONS):
         pl.semaphore_signal(
             barrier, inc=1, device_id=((sec + k) % SECTIONS, sh), device_id_type=MESH
         )
+    for k in range(1, SIDE):
+        greet(py, (px + k) % SIDE, core)
+        greet((py + k) % SIDE, px, core)
+    greet(py, px, 1 - core)
+
+    def tell_row():
+        for k in range(1, SIDE):
+            to = at(py, (px + k) % SIDE, core)
+            pl.semaphore_signal(ready.at[0], inc=1, device_id=to, device_id_type=MESH)
+
+    def tell_plane():
+        pl.semaphore_wait(ready.at[0], SIDE - 1)
+        for k in range(1, SIDE):
+            to = at((py + k) % SIDE, px, core)
+            pl.semaphore_signal(ready.at[1], inc=1, device_id=to, device_id_type=MESH)
+
+    def tell_all():
+        pl.semaphore_wait(ready.at[1], SIDE - 1)
+        lax.fori_loop(1, SHARDS, tell_ids, 0)
 
     def pool_copy(s):
         return pltpu.make_async_remote_copy(
@@ -255,9 +277,9 @@
             act[rows, cols] = (z * sig).astype(BF16)
             slope[:, cols] = sig * (1.0 + z * (1.0 - sig))
 
-    def backward(c, k, size):
+    def backward(c, start, size):
         crows = chunk_rows(c, size)
-        krows = pl.ds(k * size, size)
+        krows = pl.ds(start, size)
         for j in range(WIDTH // WIDE):
             cols = pl.ds(j * WIDE, WIDE)
             ga = jnp.dot(gbuf[crows, :], wout_t[:, cols], preferred_element_type=F32)
@@ -299,7 +321,8 @@
         cols = pl.ds(j * TILE, TILE)
         wout_t[:, cols] = wout[cols, :].T
 
-    pl.semaphore_wait(barrier, SHARDS - 1 + SECTIONS - 1)
+    pl.semaphore_wait(barrier, SECTIONS - 1 + 2 * (SIDE - 1) + 1)
+    tell_row()
 
     @pl.when(jnp.logical_not(first))
     def _():
@@ -317,7 +340,7 @@
     @pl.when(first)
     def _():
         lax.fori_loop(0, WIDTH // 64, clear, 0)
-        lax.fori_loop(1, SHARDS, tell_ids, 0)
+        tell_plane()
         row = lax.broadcasted_iota(jnp.int32, (TOK, TOK), 0)
         col = lax.broadcasted_iota(jnp.int32, (TOK, TOK), 1)
         feat = ids.shape[1]
@@ -333,6 +356,7 @@
             down = jnp.sum(jnp.where(row == col, across, 0.0), axis=1, keepdims=True)
             earlier = jnp.where((down == across) & (row < col), 1.0, 0.0)
             rank[m] = 2.0 * across + jnp.sum(earlier, axis=0, keepdims=True)
+        tell_all()
         load_pool.wait()
         for s in range(1, SECTIONS):
             pool_copy(s).wait_recv()
@@ -342,23 +366,24 @@
     def _():
         load_top(0).wait()
         for k in range(CHUNKS):
-            backward(k, k, CHUNK)
+            backward(k, k * CHUNK, CHUNK)
             relay_copy(k, CHUNK).start()
 
     @pl.when(jnp.logical_not(first))
     def _():
+        tell_plane()
         lax.fori_loop(0, WIDTH // 64, clear, 0)
-        lax.fori_loop(1, SHARDS, tell_ids, 0)
+        tell_all()
 
     all_ids[sh] = ids[...]
     send_left(0)
 
-    def step(c, k, size):
+    def step(c, start, size):
         @pl.when(jnp.logical_not(last))
         def _():
             relay_copy(c, size).wait_recv()
 
-        backward(c, k, size)
+        backward(c, start, size)
 
         @pl.when(jnp.logical_not(first))
         def _():
@@ -387,7 +412,7 @@
                 load_top(m).wait()
 
             for k in range(CHUNKS):
-                step(m * CHUNKS + k, k, CHUNK)
+                step(m * CHUNKS + k, k * CHUNK, CHUNK)
                 if k == 0:
 
                     @pl.when(m > 0)
@@ -403,20 +428,84 @@
     lax.fori_loop(0, MICRO - 1, micro_step, 0)
 
     final = MICRO - 1
-    tail = TOK - 2 * LATE
+    tail = TOK - CHUNK
+
+    def unit_copy(source, target, send, recv, k, to, came):
+        return pltpu.make_async_remote_copy(
+            src_ref=source.at[to],
+            dst_ref=target.at[came],
+            send_sem=send.at[k],
+            recv_sem=recv.at[k],
+            device_id=(sec, to),
+            device_id_type=MESH,
+        )
+
+    def soon_copy(k, to, came):
+        return unit_copy(soon, got_soon, soon_send, soon_recv, k, to, came)
+
+    def late_copy(k, to, came):
+        return unit_copy(late, got_late, late_send, late_recv, k, to, came)
+
+    def hand_soon(k, carry):
+        soon_copy(k, (sh + k) % SHARDS, sh).start()
+        return carry
+
+    def hand_late(k, carry):
+        late_copy(k, (sh + k) % SHARDS, sh).start()
+        return carry
+
+    def soon_units():
+        row = lax.broadcasted_iota(jnp.int32, (SOON, SOON), 0)
+        col = lax.broadcasted_iota(jnp.int32, (SOON, SOON), 1)
+        target = ((col >> 1) & (SHARDS - 1)) * (2 * (MICRO - 1)) + (col >> 6) * 2 + (col & 1)
+        regroup = jnp.where(row == target, 1.0, 0.0).astype(BF16)
+        by_owner = jnp.dot(regroup, routed[pl.ds(0, SOON), :], preferred_element_type=F32)
+        for b in range(8):
+            flat[pl.ds(b, SOON, stride=8), :] = by_owner[:, b * 128 : (b + 1) * 128]
+        soon[...] = flat[...].reshape(soon.shape).astype(BF16)
+        got_soon[sh] = soon[sh]
+
+    def late_units():
+        by_owner = routed[pl.ds(SOON, PER_PLANE), :].astype(F32)
+        for b in range(8):
+            flat[pl.ds(b, PER_PLANE, stride=8), :] = by_owner[:, b * 128 : (b + 1) * 128]
+        late[...] = flat[pl.ds(0, PER_PLANE * 8), :].reshape(late.shape).astype(BF16)
+        got_late[sh] = late[sh]
+
+    def to_rows(got, start, count):
+        flat[pl.ds(0, count * 8), :] = got[...].astype(F32).reshape(count * 8, 128)
+        for b in range(8):
+            out_rows[pl.ds(start, count), pl.ds(b * 128, 128)] = flat[
+                pl.ds(b, count, stride=8), :
+            ].astype(BF16)
 
     @pl.when(last)
     def _():
         load_top(final).wait()
 
-    for k in range(LATES):
-        step(EARLY + k, k, LATE)
+    for k in range(CHUNKS - 1):
+        step(final * CHUNKS + k, k * CHUNK, CHUNK)
         if k == 0:
             weight_grads(final - 1)
-        if k == LATES - 3:
+
+            @pl.when(first)
+            def _():
+                soon_units()
+        if k == 1:
+
+            @pl.when(first)
+            def _():
+                lax.fori_loop(1, SHARDS // 2, hand_soon, 0)
+        if k == 2:
             send_right(final, final * TOK, tail)
+
+            @pl.when(first)
+            def _():
+                lax.fori_loop(SHARDS // 2, SHARDS, hand_soon, 0)
+
+    for k in range(CHUNK // LATE):
+        step(EARLY + k, tail + k * LATE, LATE)
     send_right(final + 1, final * TOK + tail, TOK - tail)
-    route(final)
     own_grads(final, False)
 
     def block_rows(y, x):
@@ -436,12 +525,13 @@
             device_id_type=MESH,
         )
 
-    def y_copy(d):
-        return pltpu.make_async_remote_copy(
-            src_ref=send_y.at[d - 1],
-            dst_ref=recv_y.at[d - 1],
-            send_sem=y_send.at[d - 1],
-            recv_sem=y_recv.at[d - 1],
+    def y_copy(d, x):
+        rows = pl.ds(pl.multiple_of(x * BLOCK, BLOCK), BLOCK)
+        return pltpu.make_async_remote_copy(
+            src_ref=send_y.at[d - 1, rows],
+            dst_ref=recv_y.at[d - 1, rows],
+            send_sem=y_send.at[d - 1, x],
+            recv_sem=y_recv.at[d - 1, x],
             device_id=at((py + d) % SIDE, px, core),
             device_id_type=MESH,
         )
@@ -472,36 +562,21 @@
             x_copy(dx, y).start()
         if d != 0:
             send_y[d - 1] = total[:, HALF:].astype(BF16)
-            y_copy(d).start()
+    for e in order:
+        for d in (2, 1, 3):
+            y_copy(d, (px + e) % SIDE).start()
+    route(final)
 
     @pl.when(jnp.logical_not(first))
     def _():
-        for m in range(MICRO):
+        for m in range(MICRO - 1):
             route_copy(m, 1).wait_recv()
-
-    row = lax.broadcasted_iota(jnp.int32, (TOK, TOK), 0)
-    col = lax.broadcasted_iota(jnp.int32, (TOK, TOK), 1)
-    source = ((row >> 1) & 3) * PER_PLANE + (row >> 3) * 2 + (row & 1)
-    regroup = jnp.where(source == col, 1.0, 0.0).astype(BF16)
-    by_owner = jnp.dot(regroup, routed[...], preferred_element_type=F32)
-    spread[...] = by_owner.reshape(SHARDS, 2 * MICRO, WIDTH).astype(BF16)
-
-    def spread_copy(k, to, came):
-        return pltpu.make_async_remote_copy(
-            src_ref=spread.at[to],
-            dst_ref=out_rows.at[came],
-            send_sem=spread_send.at[k],
-            recv_sem=spread_recv.at[k],
-            device_id=(sec, to),
-            device_id_type=MESH,
-        )
-
-    def hand_out(k, carry):
-        spread_copy(k, (sh + k) % SHARDS, sh).start()
-        return carry
-
-    lax.fori_loop(1, SHARDS, hand_out, 0)
-    out_rows[sh] = spread[sh]
+        soon_units()
+        lax.fori_loop(1, SHARDS, hand_soon, 0)
+        route_copy(final, 1).wait_recv()
+
+    late_units()
+    lax.fori_loop(1, SHARDS, hand_late, 0)
 
     def hear_ids(k, carry):
         ids_copy(k, (sh + k) % SHARDS, (sh + SHARDS - k) % SHARDS).wait_recv()
@@ -522,9 +597,12 @@
         jnp.where(at_lane == 1, low & 31, jnp.where(at_lane == 2, high >> 5, high & 31)),
     )
     half = lax.broadcasted_iota(jnp.int32, (TOK, SHARDS * MICRO), 0) >> 1
-    twice = jnp.where(
-        half == lax.broadcasted_iota(jnp.int32, (TOK, SHARDS * MICRO), 1), 1.0, 0.0
-    ).astype(BF16)
+    pair = lax.broadcasted_iota(jnp.int32, (TOK, SHARDS * MICRO), 1)
+    came, micro = pair >> 2, pair & (MICRO - 1)
+    place_of = jnp.where(
+        micro < final, came * (MICRO - 1) + micro, SHARDS * (MICRO - 1) + came
+    )
+    twice = jnp.where(half == place_of, 1.0, 0.0).astype(BF16)
     both = jnp.dot(twice, parts.astype(F32).astype(BF16), preferred_element_type=F32)
     odd = lax.broadcasted_iota(jnp.int32, (TOK, 1), 0) & 1
     row_of = jnp.where(
@@ -532,13 +610,12 @@
     )
     out_named[...] = jnp.broadcast_to(row_of.astype(jnp.int32), (TOK, 128))
 
-    for d in range(1, SIDE):
-        y_copy(d).wait_recv()
     for e in order:
         y = (py + e) % SIDE
+        x = (px + e) % SIDE
         for d in range(1, SIDE):
             x_copy(d, y).wait_recv()
-        x = (px + e) % SIDE
+            y_copy(d, x).wait_recv()
         total = acc[block_rows(y, px), left_half]
         other = acc[block_rows(py, x), right_half]
         for d in range(1, SIDE):
@@ -578,11 +655,18 @@
                 total = total + recv_c[kind, h, e].astype(F32)
             out[:, cols] = total
 
-    def collect(k, carry):
-        spread_copy(k, (sh + k) % SHARDS, (sh + SHARDS - k) % SHARDS).wait_recv()
-        return carry
-
-    lax.fori_loop(1, SHARDS, collect, 0)
+    def collect_soon(k, carry):
+        soon_copy(k, (sh + k) % SHARDS, (sh + SHARDS - k) % SHARDS).wait_recv()
+        return carry
+
+    def collect_late(k, carry):
+        late_copy(k, (sh + k) % SHARDS, (sh + SHARDS - k) % SHARDS).wait_recv()
+        return carry
+
+    lax.fori_loop(1, SHARDS, collect_soon, 0)
+    to_rows(got_soon, 0, SOON)
+    lax.fori_loop(1, SHARDS, collect_late, 0)
+    to_rows(got_late, SOON, PER_PLANE)
 
     @pl.when(jnp.logical_not(first))
     def _():
@@ -606,11 +690,12 @@
             for p in range(1, SECTIONS):
                 route_copy(m, p).wait_send()
 
-    def spread_left(k, carry):
-        spread_copy(k, (sh + k) % SHARDS, sh).wait_send()
-        return carry
-
-    lax.fori_loop(1, SHARDS, spread_left, 0)
+    def units_left(k, carry):
+        soon_copy(k, (sh + k) % SHARDS, sh).wait_send()
+        late_copy(k, (sh + k) % SHARDS, sh).wait_send()
+        return carry
+
+    lax.fori_loop(1, SHARDS, units_left, 0)
 
     def ids_left(k, carry):
         ids_copy(k, (sh + k) % SHARDS, sh).wait_send()
@@ -624,9 +709,9 @@
     right_copy(final, dz, final * TOK, tail).wait_send()
     right_copy(final + 1, dz, final * TOK + tail, TOK - tail).wait_send()
     for d in range(1, SIDE):
-        y_copy(d).wait_send()
         for y in range(SIDE):
             x_copy(d, y).wait_send()
+            y_copy(d, y).wait_send()
         for h in range(2):
             for c in range(2):
                 c_copy(h, d, c, core).wait_send()
@@ -644,7 +729,7 @@
         out_shape=(
             jax.ShapeDtypeStruct((SHARE, WIDTH), F32),
             jax.ShapeDtypeStruct((SHARE, WIDTH), F32),
-            jax.ShapeDtypeStruct((SHARDS, 2 * MICRO, WIDTH), BF16),
+            jax.ShapeDtypeStruct((TOK, WIDTH), BF16),
             jax.ShapeDtypeStruct((TOK, 128), jnp.int32),
         ),
         in_specs=[pl.BlockSpec(memory_space=pltpu.SMEM)] + [anywhere] * 5 + [vmem],
@@ -666,7 +751,11 @@
             pltpu.VMEM((SHARDS,) + ids.shape, jnp.int32),
             pltpu.VMEM((MICRO, TOK, WIDTH), BF16),
             pltpu.VMEM((TOK, WIDTH), BF16),
-            pltpu.VMEM((SHARDS, 2 * MICRO, WIDTH), BF16),
+            pltpu.VMEM((SHARDS, 16 * (MICRO - 1), 128), BF16),
+            pltpu.VMEM((SHARDS, 16 * (MICRO - 1), 128), BF16),
+            pltpu.VMEM((SHARDS, 16, 128), BF16),
+            pltpu.VMEM((SHARDS, 16, 128), BF16),
+            pltpu.VMEM((SOON * 8, 128), F32),
             pltpu.VMEM((tokens, WIDTH), BF16),
             pltpu.VMEM((tokens, WIDTH), BF16),
             pltpu.VMEM((SIDE, SIDE * BLOCK, HALF), BF16),
@@ -688,14 +777,17 @@
             dma((SHARDS,)),
             dma((SHARDS,)),
             dma((SHARDS,)),
+            pltpu.SemaphoreType.REGULAR((2,)),
+            dma((SHARDS,)),
+            dma((SHARDS,)),
             dma((MICRO,)),
             dma((MICRO,)),
             dma((MICRO + 1,)),
             dma((MICRO + 1,)),
             dma((SIDE - 1, SIDE)),
             dma((SIDE - 1, SIDE)),
-            dma((SIDE - 1,)),
-            dma((SIDE - 1,)),
+            dma((SIDE - 1, SIDE)),
+            dma((SIDE - 1, SIDE)),
             dma((2, SIDE, 2)),
             dma((2, 2, SIDE)),
         ],
@@ -757,7 +849,7 @@
         w_out[0],
         jnp.transpose(feature_ids, (0, 2, 1)),
     )
-    table_grad, grad_in, grad_out = owner_sums(named, rows.reshape(TOK, WIDTH), out_in, out_out)
+    table_grad, grad_in, grad_out = owner_sums(named, rows, out_in, out_out)
     return (grad_in[None], grad_out[None], table_grad)
 
 

time: 103 us -> 101 us (0.981)
  Pallas kernels: 102 us -> 99.9 us
    pallas_call x1, Pallas kernels: 97.8 us -> 95.4 us  [relay(): pl.pallas_call(kernel, out_shape=(jax.ShapeDtypeStruct((SHARE, WIDTH), F3...]
where the time goes in v3:
time: 101 us
  Pallas kernels  99.9 us (99%)
    pallas_call x1, Pallas kernels, relay(): pl.pallas_call(kernel, out_shape=(jax.ShapeDtypeStruct((SHARE, WIDTH), F3...  95.4 us
    pallas_call x1, Pallas kernels, owner_sums(): pl.pallas_call(table_kernel, grid=(ROWS_OWN // TILE,), out_shape=(jax.Sha...  4.44 us

profile of v3, /device:TPU:1, one launch (start us, length us, event | category | flops | bytes accessed | tf_op | source)
XLA Modules:
  0.0 100.5 jit_solution(6692351058568664276)
XLA Ops:
  0.6 95.4 %relay.1 = (f32[32,1024]{1,0:T(8,128)}, f32[32,1024]{1,0:T(8,128)}, bf16[256,1024]{1,0:T(8,128)(2,1)}, s32[256,128]{1,0:T(8,128)}) custom-call(s32[4]{0:T(128)} %holder.1, bf16[1024,1024]{1,0:T(8,128)(2,1)} %bitcast.8, bf16[256,1024]{1,0:T(8,128)(2,1)} %bitcast.12, bf16[1024,1024]{1,0:T(8,128)(2,1)} %bitcast.9, bf16[1024,1024]{1,0:T(8,128)(2,1)} %bitcast.10, ...), custom_call_target="tpu_custom_call" | custom-call | flops 10737418240 | bytes 9437184 | tf_op jit(solution)/shard_map/relay/pallas_call | solution.py:727
  96.1 4.4 %owner_sums.1 = (f32[1024,1024]{1,0:T(8,128)}, f32[32,1024]{1,0:T(8,128)}, f32[32,1024]{1,0:T(8,128)}) custom-call(s32[256,128]{1,0:T(8,128)} %get-tuple-element.10.named, bf16[256,1024]{1,0:T(8,128)(2,1)} %get-tuple-element.11.rows, f32[32,1024]{1,0:T(8,128)} %get-tuple-element.12.grad_in, f32[32,1024]{1,0:T(8,128)} %get-tuple-element.13.grad_out), custom_call_target="tpu_custom_call" | custom-call | flops 536870912 | bytes 5242880 | tf_op jit(solution)/shard_map/owner_sums/pallas_call | solution.py:820

commit v4 on v3

--- a/solution.py
+++ b/solution.py
@@ -67,6 +67,10 @@
     late,
     got_late,
     flat,
+    named,
+    rows_buf,
+    grads,
+    transit,
     peer_l,
     peer_r,
     send_x,
@@ -89,6 +93,11 @@
     late_send,
     late_recv,
     ready,
+    hop_send,
+    hop_recv,
+    pass_send,
+    pass_recv,
+    out_sem,
     ids_send,
     ids_recv,
     l_send,
@@ -187,6 +196,33 @@
             device_id_type=MESH,
         )
 
+    def pool_rows(h):
+        return pl.ds(h * (TOK // 2), TOK // 2)
+
+    def hop_copy(h):
+        return pltpu.make_async_remote_copy(
+            src_ref=pooled.at[pool_rows(h)],
+            dst_ref=transit.at[pool_rows(h)],
+            send_sem=hop_send.at[h],
+            recv_sem=hop_recv.at[h],
+            device_id=(SECTIONS - 1, sh),
+            device_id_type=MESH,
+        )
+
+    def pass_copy(h):
+        return pltpu.make_async_remote_copy(
+            src_ref=transit.at[pool_rows(h)],
+            dst_ref=pbuf.at[2, pool_rows(h)],
+            send_sem=pass_send.at[h],
+            recv_sem=pass_recv.at[h],
+            device_id=(0, sh),
+            device_id_type=MESH,
+        )
+
+    def pass_pool(h):
+        hop_copy(h).wait_recv()
+        pass_copy(h).start()
+
     def relay_copy(c, size):
         rows = chunk_rows(c, size)
         return pltpu.make_async_remote_copy(
@@ -208,12 +244,12 @@
             device_id_type=MESH,
         )
 
-    def ids_copy(k, to, came):
+    def ids_copy(to, came):
         return pltpu.make_async_remote_copy(
             src_ref=ids,
             dst_ref=all_ids.at[came],
-            send_sem=ids_send.at[k],
-            recv_sem=ids_recv.at[k],
+            send_sem=ids_send,
+            recv_sem=ids_recv,
             device_id=(sec, to),
             device_id_type=MESH,
         )
@@ -258,7 +294,7 @@
         def _():
             right_copy(n, dz, start, size).start()
 
-    def forward(m):
+    def forward_open(m):
         rows = micro_rows(m)
         load_x(m).wait()
 
@@ -270,42 +306,47 @@
             extra = pbuf[slot]
             xbuf[rows, :] = (xbuf[rows, :].astype(F32) + extra.astype(F32)).astype(BF16)
 
+    def forward_tile(m, j):
+        rows = micro_rows(m)
+        cols = pl.ds(j * TILE, TILE)
+        z = jnp.dot(xbuf[rows, :], win[:, cols], preferred_element_type=F32)
+        sig = jax.nn.sigmoid(z)
+        act[rows, cols] = (z * sig).astype(BF16)
+        slope[m % 2, :, cols] = sig * (1.0 + z * (1.0 - sig))
+
+    def forward(m):
+        forward_open(m)
         for j in range(WIDTH // TILE):
-            cols = pl.ds(j * TILE, TILE)
-            z = jnp.dot(xbuf[rows, :], win[:, cols], preferred_element_type=F32)
-            sig = jax.nn.sigmoid(z)
-            act[rows, cols] = (z * sig).astype(BF16)
-            slope[:, cols] = sig * (1.0 + z * (1.0 - sig))
-
-    def backward(c, start, size):
+            forward_tile(m, j)
+
+    def backward(m, c, start, size):
         crows = chunk_rows(c, size)
         krows = pl.ds(start, size)
         for j in range(WIDTH // WIDE):
             cols = pl.ds(j * WIDE, WIDE)
             ga = jnp.dot(gbuf[crows, :], wout_t[:, cols], preferred_element_type=F32)
-            dz[crows, cols] = (ga * slope[krows, cols]).astype(BF16)
+            dz[crows, cols] = (ga * slope[m % 2, krows, cols]).astype(BF16)
         for j in range(WIDTH // WIDE):
             cols = pl.ds(j * WIDE, WIDE)
             back = jnp.dot(dz[crows, :], win_t[:, cols], preferred_element_type=F32)
             nbuf[crows, cols] = (gbuf[crows, cols].astype(F32) + back).astype(BF16)
 
-    def own_grads(m, and_peer):
+    def grad_tiles(m, tiles, and_peer):
         rows = micro_rows(m)
         for kind, left, right in ((0, xbuf, dz), (1, act, gbuf)):
 
             @pl.when(core == kind)
             def _(left=left, right=right):
-                for i in range(WIDTH // TILE):
+                for i in tiles:
                     cols = pl.ds(i * TILE, TILE)
                     total = acc[cols, :] + dot_tn(left[rows, cols], right[rows, :])
                     if and_peer:
                         total = total + dot_tn(peer_l[rows, cols], peer_r[rows, :])
                     acc[cols, :] = total
 
-    def weight_grads(m):
+    def hear_peer(m):
         left_copy(m, act).wait_recv()
         right_copy(m, dz, m * TOK, TOK).wait_recv()
-        own_grads(m, True)
 
     load_win.wait()
     for j in range(WIDTH // TILE):
@@ -324,9 +365,14 @@
     pl.semaphore_wait(barrier, SECTIONS - 1 + 2 * (SIDE - 1) + 1)
     tell_row()
 
-    @pl.when(jnp.logical_not(first))
+    @pl.when((sec == 1) | last)
     def _():
         pool_copy(sec).start()
+
+    @pl.when(sec == 2)
+    def _():
+        hop_copy(0).start()
+        hop_copy(1).start()
 
     def clear(i, carry):
         rows = pl.ds(pl.multiple_of(i * 64, 64), 64)
@@ -334,7 +380,7 @@
         return carry
 
     def tell_ids(k, carry):
-        ids_copy(k, (sh + k) % SHARDS, sh).start()
+        ids_copy((sh + k) % SHARDS, sh).start()
         return carry
 
     @pl.when(first)
@@ -358,15 +404,17 @@
             rank[m] = 2.0 * across + jnp.sum(earlier, axis=0, keepdims=True)
         tell_all()
         load_pool.wait()
-        for s in range(1, SECTIONS):
+        for s in (1, SECTIONS - 1):
             pool_copy(s).wait_recv()
+        for h in range(2):
+            pass_copy(h).wait_recv()
         forward(0)
 
     @pl.when(last)
     def _():
         load_top(0).wait()
         for k in range(CHUNKS):
-            backward(k, k * CHUNK, CHUNK)
+            backward(0, k, k * CHUNK, CHUNK)
             relay_copy(k, CHUNK).start()
 
     @pl.when(jnp.logical_not(first))
@@ -375,15 +423,19 @@
         lax.fori_loop(0, WIDTH // 64, clear, 0)
         tell_all()
 
+    @pl.when(last)
+    def _():
+        pass_pool(0)
+
     all_ids[sh] = ids[...]
     send_left(0)
 
-    def step(c, start, size):
+    def step(m, c, start, size):
         @pl.when(jnp.logical_not(last))
         def _():
             relay_copy(c, size).wait_recv()
 
-        backward(c, start, size)
+        backward(m, c, start, size)
 
         @pl.when(jnp.logical_not(first))
         def _():
@@ -405,24 +457,40 @@
             ]
 
     def micro_step(m, carry):
-        @pl.when(jnp.logical_not(last & (m == 0)))
+        @pl.when(last & (m == 1))
         def _():
-            @pl.when(last)
-            def _():
-                load_top(m).wait()
-
-            for k in range(CHUNKS):
-                step(m * CHUNKS + k, k * CHUNK, CHUNK)
+            pass_pool(1)
+
+        for k in range(CHUNKS):
+
+            @pl.when(jnp.logical_not(last & (m == 0)))
+            def _(k=k):
                 if k == 0:
 
-                    @pl.when(m > 0)
+                    @pl.when(last)
                     def _():
-                        weight_grads(m - 1)
+                        load_top(m).wait()
+
+                step(m, m * CHUNKS + k, k * CHUNK, CHUNK)
+
+            if k == 0:
+                forward_open(m + 1)
+                forward_tile(m + 1, 0)
+                forward_tile(m + 1, 1)
+            if k == 1:
+                forward_tile(m + 1, 2)
+                forward_tile(m + 1, 3)
+                send_left(m + 1)
+            if k > 0:
+
+                @pl.when(m > 0)
+                def _(k=k):
+                    if k == 1:
+                        hear_peer(m - 1)
+                    grad_tiles(m - 1, ((0,), (1, 2), (3,))[k - 1], True)
 
         send_right(m, m * TOK, TOK)
         route(m)
-        forward(m + 1)
-        send_left(m + 1)
         return carry
 
     lax.fori_loop(0, MICRO - 1, micro_step, 0)
@@ -430,29 +498,29 @@
     final = MICRO - 1
     tail = TOK - CHUNK
 
-    def unit_copy(source, target, send, recv, k, to, came):
+    def unit_copy(source, target, send, recv, to, came):
         return pltpu.make_async_remote_copy(
             src_ref=source.at[to],
             dst_ref=target.at[came],
-            send_sem=send.at[k],
-            recv_sem=recv.at[k],
+            send_sem=send,
+            recv_sem=recv,
             device_id=(sec, to),
             device_id_type=MESH,
         )
 
-    def soon_copy(k, to, came):
-        return unit_copy(soon, got_soon, soon_send, soon_recv, k, to, came)
-
-    def late_copy(k, to, came):
-        return unit_copy(late, got_late, late_send, late_recv, k, to, came)
-
     def hand_soon(k, carry):
-        soon_copy(k, (sh + k) % SHARDS, sh).start()
+        to = (sh + k) % SHARDS
+        unit_copy(soon, got_soon, soon_send, soon_recv, to, sh).start()
         return carry
 
     def hand_late(k, carry):
-        late_copy(k, (sh + k) % SHARDS, sh).start()
+        to = (sh + k) % SHARDS
+        unit_copy(late, got_late, late_send, late_recv, to, sh).start()
         return carry
+
+    def wait_all(ref, semaphore):
+        others = ref.at[pl.ds(0, SHARDS - 1)]
+        pltpu.make_async_copy(others, others, semaphore).wait()
 
     def soon_units():
         row = lax.broadcasted_iota(jnp.int32, (SOON, SOON), 0)
@@ -475,7 +543,7 @@
     def to_rows(got, start, count):
         flat[pl.ds(0, count * 8), :] = got[...].astype(F32).reshape(count * 8, 128)
         for b in range(8):
-            out_rows[pl.ds(start, count), pl.ds(b * 128, 128)] = flat[
+            rows_buf[pl.ds(start, count), pl.ds(b * 128, 128)] = flat[
                 pl.ds(b, count, stride=8), :
             ].astype(BF16)
 
@@ -484,29 +552,31 @@
         load_top(final).wait()
 
     for k in range(CHUNKS - 1):
-        step(final * CHUNKS + k, k * CHUNK, CHUNK)
+        step(final, final * CHUNKS + k, k * CHUNK, CHUNK)
         if k == 0:
-            weight_grads(final - 1)
 
             @pl.when(first)
             def _():
                 soon_units()
         if k == 1:
+            hear_peer(final - 1)
+            grad_tiles(final - 1, (0, 1), True)
 
             @pl.when(first)
             def _():
                 lax.fori_loop(1, SHARDS // 2, hand_soon, 0)
         if k == 2:
             send_right(final, final * TOK, tail)
+            grad_tiles(final - 1, (2, 3), True)
 
             @pl.when(first)
             def _():
                 lax.fori_loop(SHARDS // 2, SHARDS, hand_soon, 0)
 
     for k in range(CHUNK // LATE):
-        step(EARLY + k, tail + k * LATE, LATE)
+        step(final, EARLY + k, tail + k * LATE, LATE)
     send_right(final + 1, final * TOK + tail, TOK - tail)
-    own_grads(final, False)
+    grad_tiles(final, (0, 1, 2, 3), False)
 
     def block_rows(y, x):
         return pl.ds(pl.multiple_of((y * SIDE + x) * BLOCK, BLOCK), BLOCK)
@@ -578,11 +648,7 @@
     late_units()
     lax.fori_loop(1, SHARDS, hand_late, 0)
 
-    def hear_ids(k, carry):
-        ids_copy(k, (sh + k) % SHARDS, (sh + SHARDS - k) % SHARDS).wait_recv()
-        return carry
-
-    lax.fori_loop(1, SHARDS, hear_ids, 0)
+    wait_all(all_ids, ids_recv)
     own = sec * SHARDS + sh
     feature = own // (SECTIONS * SHARDS // ids.shape[1])
     heard = all_ids[:, :, feature, :].reshape(SHARDS * MICRO, ids.shape[2])
@@ -608,7 +674,49 @@
     row_of = jnp.where(
         odd == 0, both[:, 0:1] * 32.0 + both[:, 1:2], both[:, 2:3] * 32.0 + both[:, 3:4]
     )
-    out_named[...] = jnp.broadcast_to(row_of.astype(jnp.int32), (TOK, 128))
+    named[...] = jnp.broadcast_to(row_of.astype(jnp.int32), (TOK, 128))
+    put_named = pltpu.make_async_copy(named, out_named, out_sem.at[0])
+    put_named.start()
+
+    wait_all(all_ids, ids_send)
+    wait_all(soon, soon_send)
+
+    @pl.when((sec == 1) | last)
+    def _():
+        pool_copy(sec).wait_send()
+
+    @pl.when(sec == 2)
+    def _():
+        hop_copy(0).wait_send()
+        hop_copy(1).wait_send()
+
+    @pl.when(last)
+    def _():
+        pass_copy(0).wait_send()
+        pass_copy(1).wait_send()
+
+    @pl.when(jnp.logical_not(first))
+    def _():
+        def left(c, carry):
+            relay_copy(c, CHUNK).wait_send()
+            return carry
+
+        lax.fori_loop(0, EARLY, left, 0)
+        for c in range(EARLY, PIECES):
+            relay_copy(c, LATE).wait_send()
+
+    @pl.when(first)
+    def _():
+        for m in range(MICRO):
+            for p in range(1, SECTIONS):
+                route_copy(m, p).wait_send()
+
+    for m in range(MICRO):
+        left_copy(m, act).wait_send()
+    for m in range(final):
+        right_copy(m, dz, m * TOK, TOK).wait_send()
+    right_copy(final, dz, final * TOK, tail).wait_send()
+    right_copy(final + 1, dz, final * TOK + tail, TOK - tail).wait_send()
 
     for e in order:
         y = (py + e) % SIDE
@@ -637,86 +745,47 @@
                 else:
                     c_copy(h, e, c, core).start()
 
-    for kind, out in ((0, out_in), (1, out_out)):
-        for h, cols in ((0, left_half), (1, right_half)):
-
-            @pl.when(core == kind)
-            def _(h=h, out=out, cols=cols):
-                out[:, cols] = own_c[h]
-
-            @pl.when(core != kind)
-            def _(h=h, out=out, cols=cols, kind=kind):
-                c_copy(h, 0, 1 - kind, kind).wait_recv()
-                out[:, cols] = recv_c[kind, h, 0].astype(F32)
-
-            total = out[:, cols]
-            for e in range(1, SIDE):
-                c_copy(h, e, 0, kind).wait_recv()
-                total = total + recv_c[kind, h, e].astype(F32)
-            out[:, cols] = total
-
-    def collect_soon(k, carry):
-        soon_copy(k, (sh + k) % SHARDS, (sh + SHARDS - k) % SHARDS).wait_recv()
-        return carry
-
-    def collect_late(k, carry):
-        late_copy(k, (sh + k) % SHARDS, (sh + SHARDS - k) % SHARDS).wait_recv()
-        return carry
-
-    lax.fori_loop(1, SHARDS, collect_soon, 0)
+    wait_all(got_soon, soon_recv)
     to_rows(got_soon, 0, SOON)
-    lax.fori_loop(1, SHARDS, collect_late, 0)
+    wait_all(got_late, late_recv)
     to_rows(got_late, SOON, PER_PLANE)
-
-    @pl.when(jnp.logical_not(first))
-    def _():
-        pool_copy(sec).wait_send()
-
-        def left(c, carry):
-            relay_copy(c, CHUNK).wait_send()
-            return carry
-
-        lax.fori_loop(0, EARLY, left, 0)
-
-        def left_late(c, carry):
-            relay_copy(c, LATE).wait_send()
-            return carry
-
-        lax.fori_loop(EARLY, PIECES, left_late, 0)
-
-    @pl.when(first)
-    def _():
-        for m in range(MICRO):
-            for p in range(1, SECTIONS):
-                route_copy(m, p).wait_send()
-
-    def units_left(k, carry):
-        soon_copy(k, (sh + k) % SHARDS, sh).wait_send()
-        late_copy(k, (sh + k) % SHARDS, sh).wait_send()
-        return carry
-
-    lax.fori_loop(1, SHARDS, units_left, 0)
-
-    def ids_left(k, carry):
-        ids_copy(k, (sh + k) % SHARDS, sh).wait_send()
-        return carry
-
-    lax.fori_loop(1, SHARDS, ids_left, 0)
-    for m in range(MICRO):
-        left_copy(m, act).wait_send()
-    for m in range(final):
-        right_copy(m, dz, m * TOK, TOK).wait_send()
-    right_copy(final, dz, final * TOK, tail).wait_send()
-    right_copy(final + 1, dz, final * TOK + tail, TOK - tail).wait_send()
+    put_rows = pltpu.make_async_copy(rows_buf, out_rows, out_sem.at[1])
+    put_rows.start()
+    wait_all(late, late_send)
     for d in range(1, SIDE):
         for y in range(SIDE):
             x_copy(d, y).wait_send()
             y_copy(d, y).wait_send()
-        for h in range(2):
+
+    put_grads = []
+    for kind, out in ((0, out_in), (1, out_out)):
+        for h, cols in ((0, left_half), (1, right_half)):
+
+            @pl.when(core == kind)
+            def _(h=h, cols=cols, kind=kind):
+                grads[kind, :, cols] = own_c[h]
+
+            @pl.when(core != kind)
+            def _(h=h, cols=cols, kind=kind):
+                c_copy(h, 0, 1 - kind, kind).wait_recv()
+                grads[kind, :, cols] = recv_c[kind, h, 0].astype(F32)
+
+            total = grads[kind, :, cols]
+            for e in range(1, SIDE):
+                c_copy(h, e, 0, kind).wait_recv()
+                total = total + recv_c[kind, h, e].astype(F32)
+            grads[kind, :, cols] = total
+        put = pltpu.make_async_copy(grads.at[kind], out, out_sem.at[2 + kind])
+        put.start()
+        put_grads.append(put)
+
+    for h in range(2):
+        for d in range(1, SIDE):
             for c in range(2):
                 c_copy(h, d, c, core).wait_send()
-    for h in range(2):
         c_copy(h, 0, 1 - core, core).wait_send()
+    for put in (put_named, put_rows, *put_grads):
+        put.wait()
 
 
 def relay(holder, saved, pooled, grad_top, w_in, w_out, ids):
@@ -733,7 +802,7 @@
             jax.ShapeDtypeStruct((TOK, 128), jnp.int32),
         ),
         in_specs=[pl.BlockSpec(memory_space=pltpu.SMEM)] + [anywhere] * 5 + [vmem],
-        out_specs=(vmem, vmem, vmem, vmem),
+        out_specs=(anywhere, anywhere, anywhere, anywhere),
         scratch_shapes=[
             pltpu.VMEM((WIDTH, WIDTH), BF16),
             pltpu.VMEM((WIDTH, WIDTH), BF16),
@@ -744,7 +813,7 @@
             pltpu.VMEM((tokens, WIDTH), BF16),
             pltpu.VMEM((SECTIONS, TOK, WIDTH), BF16),
             pltpu.VMEM((tokens, WIDTH), BF16),
-            pltpu.VMEM((TOK, WIDTH), F32),
+            pltpu.VMEM((2, TOK, WIDTH), F32),
             pltpu.VMEM((tokens, WIDTH), BF16),
             pltpu.VMEM((WIDTH, WIDTH), F32),
             pltpu.VMEM((MICRO, 1, TOK), F32),
@@ -756,6 +825,10 @@
             pltpu.VMEM((SHARDS, 16, 128), BF16),
             pltpu.VMEM((SHARDS, 16, 128), BF16),
             pltpu.VMEM((SOON * 8, 128), F32),
+            pltpu.VMEM((TOK, 128), jnp.int32),
+            pltpu.VMEM((TOK, WIDTH), BF16),
+            pltpu.VMEM((2, SHARE, WIDTH), F32),
+            pltpu.VMEM((TOK, WIDTH), BF16),
             pltpu.VMEM((tokens, WIDTH), BF16),
             pltpu.VMEM((tokens, WIDTH), BF16),
             pltpu.VMEM((SIDE, SIDE * BLOCK, HALF), BF16),
@@ -773,13 +846,18 @@
             dma((PIECES,)),
             dma((MICRO, SECTIONS)),
             dma((MICRO,)),
-            dma((SHARDS,)),
-            dma((SHARDS,)),
-            dma((SHARDS,)),
-            dma((SHARDS,)),
+            dma,
+            dma,
+            dma,
+            dma,
             pltpu.SemaphoreType.REGULAR((2,)),
-            dma((SHARDS,)),
-            dma((SHARDS,)),
+            dma((2,)),
+            dma((2,)),
+            dma((2,)),
+            dma((2,)),
+            dma((4,)),
+            dma,
+            dma,
             dma((MICRO,)),
             dma((MICRO,)),
             dma((MICRO + 1,)),
@@ -803,7 +881,7 @@
 
 def table_kernel(named, rows, grad_in, grad_out, table, out_in, out_out):
     block = pl.program_id(0)
-    lane = lax.broadcasted_iota(jnp.int32, (TOK, TILE), 1) + block * TILE
+    lane = lax.broadcasted_iota(jnp.int32, (TOK, WIDE), 1) + block * WIDE
     hit = jnp.where(lane == named[:, 0:1], 1.0, 0.0).astype(BF16)
     table[...] = dot_tn(hit, rows[...])
 
@@ -819,7 +897,7 @@
 
     return pl.pallas_call(
         table_kernel,
-        grid=(ROWS_OWN // TILE,),
+        grid=(ROWS_OWN // WIDE,),
         out_shape=(
             jax.ShapeDtypeStruct((ROWS_OWN, WIDTH), F32),
             jax.ShapeDtypeStruct(grad_in.shape, F32),
@@ -827,10 +905,11 @@
         ),
         in_specs=[whole(named), whole(rows), whole(grad_in), whole(grad_out)],
         out_specs=(
-            pl.BlockSpec((TILE, WIDTH), lambda b: (b, 0)),
+            pl.BlockSpec((WIDE, WIDTH), lambda b: (b, 0)),
             whole(grad_in),
             whole(grad_out),
         ),
+        compiler_params=pltpu.CompilerParams(vmem_limit_bytes=32 * 1024 * 1024),
         cost_estimate=pl.CostEstimate(
             flops=2 * ROWS_OWN * TOK * WIDTH, bytes_accessed=5 * 2**20, transcendentals=0
         ),

time: 101 us -> 101 us (level)
  local copies, waits for them, and re-layouts: 0 us -> 3.75 us
  Pallas kernels: 99.9 us -> 96.3 us
    unnamed x0 -> x8, local copies, waits for them, and re-layouts: none -> 3.75 us
    pallas_call x1, Pallas kernels: 95.4 us -> 93.6 us  [relay(): pl.pallas_call(kernel, out_shape=(jax.ShapeDtypeStruct((SHARE, WIDTH), F3...]
    pallas_call x1, Pallas kernels: 4.44 us -> 2.64 us  [owner_sums(): pl.pallas_call(table_kernel, grid=(ROWS_OWN // WIDE,), out_shape=(jax.Sha...]
where the time goes in v4:
time: 101 us
  Pallas kernels  96.3 us (95%)
  local copies, waits for them, and re-layouts  3.75 us (4%)
    pallas_call x1, Pallas kernels, relay(): pl.pallas_call(kernel, out_shape=(jax.ShapeDtypeStruct((SHARE, WIDTH), F3...  93.6 us
    unnamed x8, local copies, waits for them, and re-layouts  3.75 us
    pallas_call x1, Pallas kernels, owner_sums(): pl.pallas_call(table_kernel, grid=(ROWS_OWN // WIDE,), out_shape=(jax.Sha...  2.64 us

profile of v4, /device:TPU:1, one launch (start us, length us, event | category | flops | bytes accessed | tf_op | source)
XLA Modules:
  0.0 100.6 jit_solution(10713870879446365388)
XLA Ops:
  0.6 93.6 %relay.1 = (f32[32,1024]{1,0:T(8,128)}, f32[32,1024]{1,0:T(8,128)}, bf16[256,1024]{1,0:T(8,128)(2,1)}, s32[256,128]{1,0:T(8,128)}) custom-call(s32[4]{0:T(128)} %holder.1, bf16[1024,1024]{1,0:T(8,128)(2,1)} %bitcast.8, bf16[256,1024]{1,0:T(8,128)(2,1)} %bitcast.12, bf16[1024,1024]{1,0:T(8,128)(2,1)} %bitcast.9, bf16[1024,1024]{1,0:T(8,128)(2,1)} %bitcast.10, ...), custom_call_target="tpu_custom_call" | custom-call | flops 10737418240 | bytes 9437184 | tf_op jit(solution)/shard_map/relay/pallas_call | solution.py:796
  94.3 0.0 copy-start
  94.3 1.0 %copy-done = bf16[256,1024]{1,0:T(8,128)(2,1)S(1)} copy-done((bf16[256,1024]{1,0:T(8,128)(2,1)S(1)}, bf16[256,1024]{1,0:T(8,128)(2,1)}, u32[]{:S(2)}) %copy-start) | copy-done | bytes 524312
  95.3 0.0 copy-start.1
  95.3 0.9 copy-done.1
  96.2 0.0 copy-start.2
  96.2 0.9 copy-done.2
  97.1 0.0 copy-start.3
  97.1 0.9 copy-done.3
  98.0 2.6 %owner_sums.1 = (f32[1024,1024]{1,0:T(8,128)}, f32[32,1024]{1,0:T(8,128)}, f32[32,1024]{1,0:T(8,128)}) custom-call(s32[256,128]{1,0:T(8,128)S(1)} %copy-done.3, bf16[256,1024]{1,0:T(8,128)(2,1)S(1)} %copy-done, f32[32,1024]{1,0:T(8,128)S(1)} %copy-done.1, f32[32,1024]{1,0:T(8,128)S(1)} %copy-done.2), custom_call_target="tpu_custom_call" | custom-call | flops 536870912 | bytes 5242880 | tf_op jit(solution)/shard_map/owner_sums/pallas_call | solution.py:898
Async XLA Ops:
  94.3 1.0 %copy-start = (bf16[256,1024]{1,0:T(8,128)(2,1)S(1)}, bf16[256,1024]{1,0:T(8,128)(2,1)}, u32[]{:S(2)}) copy-start(bf16[256,1024]{1,0:T(8,128)(2,1)} %get-tuple-element.11.rows) | copy-start | bytes 1572868
  95.3 0.9 copy-start.1
  96.2 0.9 copy-start.2
  97.1 0.9 copy-start.3

commit v5 on v4

--- a/solution.py
+++ b/solution.py
@@ -16,15 +16,15 @@
 MICRO = 4
 TOK = 256
 CHUNK = 64
-LATE = 32
+PIECE = 32
 WIDTH = 1024
 SHARE = WIDTH // SHARDS
 PER_PLANE = TOK // SECTIONS
 TILE = 256
 WIDE = 512
 CHUNKS = TOK // CHUNK
-EARLY = MICRO * CHUNKS - 1
-PIECES = EARLY + CHUNK // LATE
+SPLIT = CHUNK // PIECE
+PIECES = MICRO * TOK // PIECE
 SOON = (MICRO - 1) * PER_PLANE
 HALF = WIDTH // 2
 BLOCK = 2 * SHARE
@@ -125,8 +125,7 @@
     def micro_rows(m):
         return pl.ds(pl.multiple_of(m * TOK, TOK), TOK)
 
-    def chunk_rows(c, size):
-        start = c * CHUNK if size == CHUNK else EARLY * CHUNK + (c - EARLY) * LATE
+    def token_rows(start, size):
         return pl.ds(pl.multiple_of(start, size), size)
 
     def load_x(m):
@@ -223,8 +222,8 @@
         hop_copy(h).wait_recv()
         pass_copy(h).start()
 
-    def relay_copy(c, size):
-        rows = chunk_rows(c, size)
+    def relay_copy(c):
+        rows = token_rows(c * PIECE, PIECE)
         return pltpu.make_async_remote_copy(
             src_ref=nbuf.at[rows],
             dst_ref=gbuf.at[rows],
@@ -319,8 +318,8 @@
         for j in range(WIDTH // TILE):
             forward_tile(m, j)
 
-    def backward(m, c, start, size):
-        crows = chunk_rows(c, size)
+    def backward(m, start, size):
+        crows = token_rows(m * TOK + start, size)
         krows = pl.ds(start, size)
         for j in range(WIDTH // WIDE):
             cols = pl.ds(j * WIDE, WIDE)
@@ -414,8 +413,9 @@
     def _():
         load_top(0).wait()
         for k in range(CHUNKS):
-            backward(0, k, k * CHUNK, CHUNK)
-            relay_copy(k, CHUNK).start()
+            backward(0, k * CHUNK, CHUNK)
+            for i in range(SPLIT):
+                relay_copy(k * SPLIT + i).start()
 
     @pl.when(jnp.logical_not(first))
     def _():
@@ -430,16 +430,42 @@
     all_ids[sh] = ids[...]
     send_left(0)
 
-    def step(m, c, start, size):
+    def step(m, start, size):
+        pieces = [(m * TOK + start) // PIECE + i for i in range(size // PIECE)]
+
         @pl.when(jnp.logical_not(last))
         def _():
-            relay_copy(c, size).wait_recv()
-
-        backward(m, c, start, size)
+            for c in pieces:
+                relay_copy(c).wait_recv()
+
+        backward(m, start, size)
 
         @pl.when(jnp.logical_not(first))
         def _():
-            relay_copy(c, size).start()
+            for c in pieces:
+                relay_copy(c).start()
+
+    inner = jnp.logical_not(first | last)
+
+    def chunks(m, slots, final_one):
+        for k in range(CHUNKS):
+            fine = final_one and k == CHUNKS - 1
+            for i in range(SPLIT):
+
+                def piece(k=k, i=i):
+                    step(m, k * CHUNK + i * PIECE, PIECE)
+
+                if fine:
+                    piece()
+                else:
+                    pl.when(inner)(piece)
+                if not fine and i == SPLIT - 1:
+
+                    @pl.when(first | (last & (m > 0)))
+                    def _(k=k):
+                        step(m, k * CHUNK, CHUNK)
+
+                slots[k * SPLIT + i]()
 
     def route(m):
         rows = micro_rows(m)
@@ -457,38 +483,36 @@
             ]
 
     def micro_step(m, carry):
-        @pl.when(last & (m == 1))
+        @pl.when(last & (m == 2))
         def _():
             pass_pool(1)
 
-        for k in range(CHUNKS):
-
-            @pl.when(jnp.logical_not(last & (m == 0)))
-            def _(k=k):
-                if k == 0:
-
-                    @pl.when(last)
-                    def _():
-                        load_top(m).wait()
-
-                step(m, m * CHUNKS + k, k * CHUNK, CHUNK)
-
-            if k == 0:
-                forward_open(m + 1)
-                forward_tile(m + 1, 0)
-                forward_tile(m + 1, 1)
-            if k == 1:
-                forward_tile(m + 1, 2)
-                forward_tile(m + 1, 3)
-                send_left(m + 1)
-            if k > 0:
-
+        @pl.when(last & (m > 0))
+        def _():
+            load_top(m).wait()
+
+        def forward_slot(j):
+            def work():
+                if j == 0:
+                    forward_open(m + 1)
+                forward_tile(m + 1, j)
+                if j == WIDTH // TILE - 1:
+                    send_left(m + 1)
+
+            return work
+
+        def grad_slot(i):
+            def work():
                 @pl.when(m > 0)
-                def _(k=k):
-                    if k == 1:
+                def _():
+                    if i == 0:
                         hear_peer(m - 1)
-                    grad_tiles(m - 1, ((0,), (1, 2), (3,))[k - 1], True)
-
+                    grad_tiles(m - 1, (i,), True)
+
+            return work
+
+        tiles = range(WIDTH // TILE)
+        chunks(m, [forward_slot(j) for j in tiles] + [grad_slot(i) for i in tiles], False)
         send_right(m, m * TOK, TOK)
         route(m)
         return carry
@@ -551,30 +575,27 @@
     def _():
         load_top(final).wait()
 
-    for k in range(CHUNKS - 1):
-        step(final, final * CHUNKS + k, k * CHUNK, CHUNK)
-        if k == 0:
+    def final_slot(n):
+        def work():
+            if n == 1:
+                hear_peer(final - 1)
+            if 1 <= n <= WIDTH // TILE:
+                grad_tiles(final - 1, (n - 1,), True)
+            if n == 5:
+                send_right(final, final * TOK, tail)
 
             @pl.when(first)
             def _():
-                soon_units()
-        if k == 1:
-            hear_peer(final - 1)
-            grad_tiles(final - 1, (0, 1), True)
-
-            @pl.when(first)
-            def _():
-                lax.fori_loop(1, SHARDS // 2, hand_soon, 0)
-        if k == 2:
-            send_right(final, final * TOK, tail)
-            grad_tiles(final - 1, (2, 3), True)
-
-            @pl.when(first)
-            def _():
-                lax.fori_loop(SHARDS // 2, SHARDS, hand_soon, 0)
-
-    for k in range(CHUNK // LATE):
-        step(final, EARLY + k, tail + k * LATE, LATE)
+                if n == 0:
+                    soon_units()
+                if n == 2:
+                    lax.fori_loop(1, SHARDS // 2, hand_soon, 0)
+                if n == 4:
+                    lax.fori_loop(SHARDS // 2, SHARDS, hand_soon, 0)
+
+        return work
+
+    chunks(final, [final_slot(n) for n in range(CHUNKS * SPLIT)], True)
     send_right(final + 1, final * TOK + tail, TOK - tail)
     grad_tiles(final, (0, 1, 2, 3), False)
 
@@ -698,16 +719,14 @@
     @pl.when(jnp.logical_not(first))
     def _():
         def left(c, carry):
-            relay_copy(c, CHUNK).wait_send()
+            relay_copy(c).wait_send()
             return carry
 
-        lax.fori_loop(0, EARLY, left, 0)
-        for c in range(EARLY, PIECES):
-            relay_copy(c, LATE).wait_send()
+        lax.fori_loop(0, PIECES, left, 0)
 
     @pl.when(first)
     def _():
-        for m in range(MICRO):
+        for m in range(final):
             for p in range(1, SECTIONS):
                 route_copy(m, p).wait_send()
 
@@ -752,6 +771,12 @@
     put_rows = pltpu.make_async_copy(rows_buf, out_rows, out_sem.at[1])
     put_rows.start()
     wait_all(late, late_send)
+
+    @pl.when(first)
+    def _():
+        for p in range(1, SECTIONS):
+            route_copy(final, p).wait_send()
+
     for d in range(1, SIDE):
         for y in range(SIDE):
             x_copy(d, y).wait_send()

time: 101 us -> 97.7 us (0.967)
  Pallas kernels: 96.3 us -> 93 us
    pallas_call x1, Pallas kernels: 93.6 us -> 90.4 us  [relay(): pl.pallas_call(kernel, out_shape=(jax.ShapeDtypeStruct((SHARE, WIDTH), F3...]
where the time goes in v5:
time: 97.7 us; the launch traced here: 97.4 us
  Pallas kernels  93 us (95%)
  local copies, waits for them, and re-layouts  3.75 us (4%)
    pallas_call x1, Pallas kernels, relay(): pl.pallas_call(kernel, out_shape=(jax.ShapeDtypeStruct((SHARE, WIDTH), F3...  90.4 us
    unnamed x8, local copies, waits for them, and re-layouts  3.75 us
    pallas_call x1, Pallas kernels, owner_sums(): pl.pallas_call(table_kernel, grid=(ROWS_OWN // WIDE,), out_shape=(jax.Sha...  2.64 us

profile of v5, /device:TPU:1, one launch (start us, length us, event | category | flops | bytes accessed | tf_op | source)
XLA Modules:
  0.0 97.4 jit_solution(13651843266574283924)
XLA Ops:
  0.6 90.4 %relay.1 = (f32[32,1024]{1,0:T(8,128)}, f32[32,1024]{1,0:T(8,128)}, bf16[256,1024]{1,0:T(8,128)(2,1)}, s32[256,128]{1,0:T(8,128)}) custom-call(s32[4]{0:T(128)} %holder.1, bf16[1024,1024]{1,0:T(8,128)(2,1)} %bitcast.8, bf16[256,1024]{1,0:T(8,128)(2,1)} %bitcast.12, bf16[1024,1024]{1,0:T(8,128)(2,1)} %bitcast.9, bf16[1024,1024]{1,0:T(8,128)(2,1)} %bitcast.10, ...), custom_call_target="tpu_custom_call" | custom-call | flops 10737418240 | bytes 9437184 | tf_op jit(solution)/shard_map/relay/pallas_call | solution.py:821
  91.0 0.0 copy-start
  91.0 1.0 %copy-done = bf16[256,1024]{1,0:T(8,128)(2,1)S(1)} copy-done((bf16[256,1024]{1,0:T(8,128)(2,1)S(1)}, bf16[256,1024]{1,0:T(8,128)(2,1)}, u32[]{:S(2)}) %copy-start) | copy-done | bytes 524312
  92.1 0.0 copy-start.1
  92.1 0.9 copy-done.1
  93.0 0.0 copy-start.2
  93.0 0.9 copy-done.2
  93.9 0.0 copy-start.3
  93.9 0.9 copy-done.3
  94.8 2.6 %owner_sums.1 = (f32[1024,1024]{1,0:T(8,128)}, f32[32,1024]{1,0:T(8,128)}, f32[32,1024]{1,0:T(8,128)}) custom-call(s32[256,128]{1,0:T(8,128)S(1)} %copy-done.3, bf16[256,1024]{1,0:T(8,128)(2,1)S(1)} %copy-done, f32[32,1024]{1,0:T(8,128)S(1)} %copy-done.1, f32[32,1024]{1,0:T(8,128)S(1)} %copy-done.2), custom_call_target="tpu_custom_call" | custom-call | flops 536870912 | bytes 5242880 | tf_op jit(solution)/shard_map/owner_sums/pallas_call | solution.py:923
Async XLA Ops:
  91.0 1.0 %copy-start = (bf16[256,1024]{1,0:T(8,128)(2,1)S(1)}, bf16[256,1024]{1,0:T(8,128)(2,1)}, u32[]{:S(2)}) copy-start(bf16[256,1024]{1,0:T(8,128)(2,1)} %get-tuple-element.11.rows) | copy-start | bytes 1572868
  92.1 0.9 copy-start.1
  93.0 0.9 copy-start.2
  93.9 0.9 copy-start.3

commit v6 on v5

--- a/solution.py
+++ b/solution.py
@@ -146,11 +146,7 @@
 
     @pl.when(last)
     def _():
-        for m in range(MICRO):
-            load_top(m).start()
-
-    for m in range(1, MICRO):
-        load_x(m).start()
+        load_top(0).start()
 
     @pl.when(first)
     def _():
@@ -372,6 +368,22 @@
     def _():
         hop_copy(0).start()
         hop_copy(1).start()
+
+    @pl.when(last)
+    def _():
+        load_top(0).wait()
+        for i in range(SPLIT):
+            backward(0, i * PIECE, PIECE)
+            relay_copy(i).start()
+        for k in range(1, CHUNKS):
+            backward(0, k * CHUNK, CHUNK)
+            for i in range(SPLIT):
+                relay_copy(k * SPLIT + i).start()
+        for m in range(1, MICRO):
+            load_top(m).start()
+
+    for m in range(1, MICRO):
+        load_x(m).start()
 
     def clear(i, carry):
         rows = pl.ds(pl.multiple_of(i * 64, 64), 64)
@@ -409,14 +421,6 @@
             pass_copy(h).wait_recv()
         forward(0)
 
-    @pl.when(last)
-    def _():
-        load_top(0).wait()
-        for k in range(CHUNKS):
-            backward(0, k * CHUNK, CHUNK)
-            for i in range(SPLIT):
-                relay_copy(k * SPLIT + i).start()
-
     @pl.when(jnp.logical_not(first))
     def _():
         tell_plane()
@@ -430,7 +434,7 @@
     all_ids[sh] = ids[...]
     send_left(0)
 
-    def step(m, start, size):
+    def step(m, start, size, hook=None):
         pieces = [(m * TOK + start) // PIECE + i for i in range(size // PIECE)]
 
         @pl.when(jnp.logical_not(last))
@@ -438,6 +442,8 @@
             for c in pieces:
                 relay_copy(c).wait_recv()
 
+        if hook is not None:
+            hook()
         backward(m, start, size)
 
         @pl.when(jnp.logical_not(first))
@@ -447,13 +453,14 @@
 
     inner = jnp.logical_not(first | last)
 
-    def chunks(m, slots, final_one):
+    def chunks(m, slots, hook=None):
         for k in range(CHUNKS):
-            fine = final_one and k == CHUNKS - 1
+            fine = hook is not None and k == CHUNKS - 1
             for i in range(SPLIT):
 
                 def piece(k=k, i=i):
-                    step(m, k * CHUNK + i * PIECE, PIECE)
+                    at_last = hook if fine and i == SPLIT - 1 else None
+                    step(m, k * CHUNK + i * PIECE, PIECE, at_last)
 
                 if fine:
                     piece()
@@ -512,7 +519,7 @@
             return work
 
         tiles = range(WIDTH // TILE)
-        chunks(m, [forward_slot(j) for j in tiles] + [grad_slot(i) for i in tiles], False)
+        chunks(m, [forward_slot(j) for j in tiles] + [grad_slot(i) for i in tiles])
         send_right(m, m * TOK, TOK)
         route(m)
         return carry
@@ -577,10 +584,10 @@
 
     def final_slot(n):
         def work():
-            if n == 1:
+            if n == 2:
                 hear_peer(final - 1)
-            if 1 <= n <= WIDTH // TILE:
-                grad_tiles(final - 1, (n - 1,), True)
+            if 2 <= n < 2 + WIDTH // TILE:
+                grad_tiles(final - 1, (n - 2,), True)
             if n == 5:
                 send_right(final, final * TOK, tail)
 
@@ -595,8 +602,17 @@
 
         return work
 
-    chunks(final, [final_slot(n) for n in range(CHUNKS * SPLIT)], True)
-    send_right(final + 1, final * TOK + tail, TOK - tail)
+    def hand_g():
+        @pl.when(core == 0)
+        def _():
+            right_copy(final + 1, gbuf, final * TOK + tail, TOK - tail).start()
+
+    chunks(final, [final_slot(n) for n in range(CHUNKS * SPLIT)], hand_g)
+
+    @pl.when(core == 1)
+    def _():
+        right_copy(final + 1, dz, final * TOK + tail, TOK - tail).start()
+
     grad_tiles(final, (0, 1, 2, 3), False)
 
     def block_rows(y, x):

time: 97.7 us -> 96.5 us (0.988)
  Pallas kernels: 93 us -> 91.9 us
    pallas_call x1, Pallas kernels: 90.4 us -> 89.2 us  [relay(): pl.pallas_call(kernel, out_shape=(jax.ShapeDtypeStruct((SHARE, WIDTH), F3...]
where the time goes in v6:
time: 96.5 us; the launch traced here: 96.3 us
  Pallas kernels  91.9 us (95%)
  local copies, waits for them, and re-layouts  3.75 us (4%)
    pallas_call x1, Pallas kernels, relay(): pl.pallas_call(kernel, out_shape=(jax.ShapeDtypeStruct((SHARE, WIDTH), F3...  89.2 us
    unnamed x8, local copies, waits for them, and re-layouts  3.75 us
    pallas_call x1, Pallas kernels, owner_sums(): pl.pallas_call(table_kernel, grid=(ROWS_OWN // WIDE,), out_shape=(jax.Sha...  2.64 us

profile of v6, /device:TPU:1, one launch (start us, length us, event | category | flops | bytes accessed | tf_op | source)
XLA Modules:
  0.0 96.3 jit_solution(2108544889518276592)
XLA Ops:
  0.6 89.2 %relay.1 = (f32[32,1024]{1,0:T(8,128)}, f32[32,1024]{1,0:T(8,128)}, bf16[256,1024]{1,0:T(8,128)(2,1)}, s32[256,128]{1,0:T(8,128)}) custom-call(s32[4]{0:T(128)} %holder.1, bf16[1024,1024]{1,0:T(8,128)(2,1)} %bitcast.8, bf16[256,1024]{1,0:T(8,128)(2,1)} %bitcast.12, bf16[1024,1024]{1,0:T(8,128)(2,1)} %bitcast.9, bf16[1024,1024]{1,0:T(8,128)(2,1)} %bitcast.10, ...), custom_call_target="tpu_custom_call" | custom-call | flops 10737418240 | bytes 9437184 | tf_op jit(solution)/shard_map/relay/pallas_call | solution.py:837
  89.9 0.0 copy-start
  89.9 1.0 %copy-done = bf16[256,1024]{1,0:T(8,128)(2,1)S(1)} copy-done((bf16[256,1024]{1,0:T(8,128)(2,1)S(1)}, bf16[256,1024]{1,0:T(8,128)(2,1)}, u32[]{:S(2)}) %copy-start) | copy-done | bytes 524312
  90.9 0.0 copy-start.1
  90.9 0.9 copy-done.1
  91.8 0.0 copy-start.2
  91.8 0.9 copy-done.2
  92.7 0.0 copy-start.3
  92.7 0.9 copy-done.3
  93.6 2.6 %owner_sums.1 = (f32[1024,1024]{1,0:T(8,128)}, f32[32,1024]{1,0:T(8,128)}, f32[32,1024]{1,0:T(8,128)}) custom-call(s32[256,128]{1,0:T(8,128)S(1)} %copy-done.3, bf16[256,1024]{1,0:T(8,128)(2,1)S(1)} %copy-done, f32[32,1024]{1,0:T(8,128)S(1)} %copy-done.1, f32[32,1024]{1,0:T(8,128)S(1)} %copy-done.2), custom_call_target="tpu_custom_call" | custom-call | flops 536870912 | bytes 5242880 | tf_op jit(solution)/shard_map/owner_sums/pallas_call | solution.py:939
Async XLA Ops:
  89.9 1.0 %copy-start = (bf16[256,1024]{1,0:T(8,128)(2,1)S(1)}, bf16[256,1024]{1,0:T(8,128)(2,1)}, u32[]{:S(2)}) copy-start(bf16[256,1024]{1,0:T(8,128)(2,1)} %get-tuple-element.11.rows) | copy-start | bytes 1572868
  90.9 0.9 copy-start.1
  91.8 0.9 copy-start.2
  92.7 0.9 copy-start.3

commit v7 on v6

--- a/solution.py
+++ b/solution.py
@@ -42,8 +42,7 @@
     w_in,
     w_out,
     ids,
-    out_in,
-    out_out,
+    out_parts,
     out_rows,
     out_named,
     win,
@@ -69,7 +68,6 @@
     flat,
     named,
     rows_buf,
-    grads,
     transit,
     peer_l,
     peer_r,
@@ -77,9 +75,7 @@
     recv_x,
     send_y,
     recv_y,
-    own_c,
     send_c,
-    recv_c,
     load_sem,
     top_sem,
     pool_send,
@@ -177,9 +173,22 @@
             to = at((py + k) % SIDE, px, core)
             pl.semaphore_signal(ready.at[1], inc=1, device_id=to, device_id_type=MESH)
 
-    def tell_all():
-        pl.semaphore_wait(ready.at[1], SIDE - 1)
-        lax.fori_loop(1, SHARDS, tell_ids, 0)
+    def tell_ids(m, n):
+        if n == 0:
+
+            @pl.when(m == 0)
+            def _():
+                tell_plane()
+
+        if n == 1:
+
+            @pl.when(m == 0)
+            def _():
+                pl.semaphore_wait(ready.at[1], SIDE - 1)
+
+        @pl.when((m > 0) | (n > 0))
+        def _():
+            ids_copy((sh + m * SPLIT * CHUNKS + n) % SHARDS, sh).start()
 
     def pool_copy(s):
         return pltpu.make_async_remote_copy(
@@ -390,14 +399,9 @@
         acc[rows, :] = jnp.zeros((64, WIDTH), F32)
         return carry
 
-    def tell_ids(k, carry):
-        ids_copy((sh + k) % SHARDS, sh).start()
-        return carry
-
     @pl.when(first)
     def _():
         lax.fori_loop(0, WIDTH // 64, clear, 0)
-        tell_plane()
         row = lax.broadcasted_iota(jnp.int32, (TOK, TOK), 0)
         col = lax.broadcasted_iota(jnp.int32, (TOK, TOK), 1)
         feat = ids.shape[1]
@@ -413,7 +417,6 @@
             down = jnp.sum(jnp.where(row == col, across, 0.0), axis=1, keepdims=True)
             earlier = jnp.where((down == across) & (row < col), 1.0, 0.0)
             rank[m] = 2.0 * across + jnp.sum(earlier, axis=0, keepdims=True)
-        tell_all()
         load_pool.wait()
         for s in (1, SECTIONS - 1):
             pool_copy(s).wait_recv()
@@ -423,9 +426,7 @@
 
     @pl.when(jnp.logical_not(first))
     def _():
-        tell_plane()
         lax.fori_loop(0, WIDTH // 64, clear, 0)
-        tell_all()
 
     @pl.when(last)
     def _():
@@ -473,6 +474,7 @@
                         step(m, k * CHUNK, CHUNK)
 
                 slots[k * SPLIT + i]()
+                tell_ids(m, k * SPLIT + i)
 
     def route(m):
         rows = micro_rows(m)
@@ -647,11 +649,16 @@
         there = (py + e) % SIDE if h == 0 else (px + e) % SIDE
         return pltpu.make_async_remote_copy(
             src_ref=send_c.at[h, e, c],
-            dst_ref=recv_c.at[kind, h, e],
+            dst_ref=out_parts.at[kind, h, e],
             send_sem=c_send.at[h, e, c],
             recv_sem=c_recv.at[kind, h, e],
             device_id=at(there, px, c) if h == 0 else at(py, there, c),
             device_id_type=MESH,
+        )
+
+    def own_part(h):
+        return pltpu.make_async_copy(
+            send_c.at[h, 0, core], out_parts.at[core, h, 0], out_sem.at[2 + h]
         )
 
     order = (2, 1, 3, 0)
@@ -771,8 +778,8 @@
                 if e == 0:
 
                     @pl.when(core == c)
-                    def _(h=h, c=c, part=part):
-                        own_c[h] = part[c * SHARE : (c + 1) * SHARE, :]
+                    def _(h=h, c=c):
+                        own_part(h).start()
 
                     @pl.when(core != c)
                     def _(h=h, c=c):
@@ -798,34 +805,22 @@
             x_copy(d, y).wait_send()
             y_copy(d, y).wait_send()
 
-    put_grads = []
-    for kind, out in ((0, out_in), (1, out_out)):
-        for h, cols in ((0, left_half), (1, right_half)):
-
-            @pl.when(core == kind)
-            def _(h=h, cols=cols, kind=kind):
-                grads[kind, :, cols] = own_c[h]
+    for kind in range(2):
+        for h in range(2):
 
             @pl.when(core != kind)
-            def _(h=h, cols=cols, kind=kind):
+            def _(h=h, kind=kind):
                 c_copy(h, 0, 1 - kind, kind).wait_recv()
-                grads[kind, :, cols] = recv_c[kind, h, 0].astype(F32)
-
-            total = grads[kind, :, cols]
+
             for e in range(1, SIDE):
                 c_copy(h, e, 0, kind).wait_recv()
-                total = total + recv_c[kind, h, e].astype(F32)
-            grads[kind, :, cols] = total
-        put = pltpu.make_async_copy(grads.at[kind], out, out_sem.at[2 + kind])
-        put.start()
-        put_grads.append(put)
 
     for h in range(2):
         for d in range(1, SIDE):
             for c in range(2):
                 c_copy(h, d, c, core).wait_send()
         c_copy(h, 0, 1 - core, core).wait_send()
-    for put in (put_named, put_rows, *put_grads):
+    for put in (put_named, put_rows, own_part(0), own_part(1)):
         put.wait()
 
 
@@ -837,13 +832,12 @@
     return pl.pallas_call(
         kernel,
         out_shape=(
-            jax.ShapeDtypeStruct((SHARE, WIDTH), F32),
-            jax.ShapeDtypeStruct((SHARE, WIDTH), F32),
+            jax.ShapeDtypeStruct((2, 2, SIDE, SHARE, HALF), BF16),
             jax.ShapeDtypeStruct((TOK, WIDTH), BF16),
             jax.ShapeDtypeStruct((TOK, 128), jnp.int32),
         ),
         in_specs=[pl.BlockSpec(memory_space=pltpu.SMEM)] + [anywhere] * 5 + [vmem],
-        out_specs=(anywhere, anywhere, anywhere, anywhere),
+        out_specs=(anywhere, anywhere, anywhere),
         scratch_shapes=[
             pltpu.VMEM((WIDTH, WIDTH), BF16),
             pltpu.VMEM((WIDTH, WIDTH), BF16),
@@ -868,7 +862,6 @@
             pltpu.VMEM((SOON * 8, 128), F32),
             pltpu.VMEM((TOK, 128), jnp.int32),
             pltpu.VMEM((TOK, WIDTH), BF16),
-            pltpu.VMEM((2, SHARE, WIDTH), F32),
             pltpu.VMEM((TOK, WIDTH), BF16),
             pltpu.VMEM((tokens, WIDTH), BF16),
             pltpu.VMEM((tokens, WIDTH), BF16),
@@ -876,9 +869,7 @@
             pltpu.VMEM((SIDE - 1, SIDE, BLOCK, HALF), BF16),
             pltpu.VMEM((SIDE - 1, SIDE * BLOCK, HALF), BF16),
             pltpu.VMEM((SIDE - 1, SIDE * BLOCK, HALF), BF16),
-            pltpu.VMEM((2, SHARE, HALF), F32),
             pltpu.VMEM((2, SIDE, 2, SHARE, HALF), BF16),
-            pltpu.VMEM((2, 2, SIDE, SHARE, HALF), BF16),
             dma((3 + MICRO,)),
             dma((MICRO,)),
             dma,
@@ -920,7 +911,7 @@
     )(holder, saved, pooled, grad_top, w_in, w_out, ids)
 
 
-def table_kernel(named, rows, grad_in, grad_out, table, out_in, out_out):
+def table_kernel(named, rows, parts, table, out_in, out_out):
     block = pl.program_id(0)
     lane = lax.broadcasted_iota(jnp.int32, (TOK, WIDE), 1) + block * WIDE
     hit = jnp.where(lane == named[:, 0:1], 1.0, 0.0).astype(BF16)
@@ -928,39 +919,40 @@
 
     @pl.when(block == 0)
     def _():
-        out_in[...] = grad_in[...]
-        out_out[...] = grad_out[...]
-
-
-def owner_sums(named, rows, grad_in, grad_out):
-    def whole(array):
-        return pl.BlockSpec(array.shape, lambda b: (0, 0))
-
+        for kind, out in ((0, out_in), (1, out_out)):
+            for h in range(2):
+                total = parts[kind, h, 0].astype(F32)
+                for e in range(1, SIDE):
+                    total = total + parts[kind, h, e].astype(F32)
+                out[:, h * HALF : (h + 1) * HALF] = total
+
+
+def owner_sums(named, rows, parts):
+    def whole(shape):
+        return pl.BlockSpec(shape, lambda b: (0,) * len(shape))
+
+    share = jax.ShapeDtypeStruct((SHARE, WIDTH), F32)
     return pl.pallas_call(
         table_kernel,
         grid=(ROWS_OWN // WIDE,),
-        out_shape=(
-            jax.ShapeDtypeStruct((ROWS_OWN, WIDTH), F32),
-            jax.ShapeDtypeStruct(grad_in.shape, F32),
-            jax.ShapeDtypeStruct(grad_out.shape, F32),
-        ),
-        in_specs=[whole(named), whole(rows), whole(grad_in), whole(grad_out)],
+        out_shape=(jax.ShapeDtypeStruct((ROWS_OWN, WIDTH), F32), share, share),
+        in_specs=[whole(named.shape), whole(rows.shape), whole(parts.shape)],
         out_specs=(
             pl.BlockSpec((WIDE, WIDTH), lambda b: (b, 0)),
-            whole(grad_in),
-            whole(grad_out),
+            whole(share.shape),
+            whole(share.shape),
         ),
         compiler_params=pltpu.CompilerParams(vmem_limit_bytes=32 * 1024 * 1024),
         cost_estimate=pl.CostEstimate(
             flops=2 * ROWS_OWN * TOK * WIDTH, bytes_accessed=5 * 2**20, transcendentals=0
         ),
         name="owner_sums",
-    )(named, rows, grad_in, grad_out)
+    )(named, rows, parts)
 
 
 def local(saved, pooled, grad_top, w_in, w_out, feature_ids, holder_order):
     tokens = MICRO * TOK
-    out_in, out_out, rows, named = relay(
+    parts, rows, named = relay(
         holder_order,
         saved.reshape(tokens, WIDTH),
         pooled.reshape(TOK, WIDTH),
@@ -969,7 +961,7 @@
         w_out[0],
         jnp.transpose(feature_ids, (0, 2, 1)),
     )
-    table_grad, grad_in, grad_out = owner_sums(named, rows, out_in, out_out)
+    table_grad, grad_in, grad_out = owner_sums(named, rows, parts)
     return (grad_in[None], grad_out[None], table_grad)
 
 

time: 96.5 us -> 95.6 us (level)
    unnamed x8 -> x6, local copies, waits for them, and re-layouts: 3.75 us -> 2.98 us
where the time goes in v7:
time: 95.6 us; the launch traced here: 95.4 us
  Pallas kernels  91.7 us (96%)
  local copies, waits for them, and re-layouts  2.98 us (3%)
    pallas_call x1, Pallas kernels, relay(): pl.pallas_call(kernel, out_shape=(jax.ShapeDtypeStruct((2, 2, SIDE, SHARE...  89 us
    unnamed x6, local copies, waits for them, and re-layouts  2.98 us
    pallas_call x1, Pallas kernels, owner_sums(): pl.pallas_call(table_kernel, grid=(ROWS_OWN // WIDE,), out_shape=(jax.Sha...  2.68 us

profile of v7, /device:TPU:1, one launch (start us, length us, event | category | flops | bytes accessed | tf_op | source)
XLA Modules:
  0.0 95.4 jit_solution(2023118231739788167)
XLA Ops:
  0.6 89.0 %relay.1 = (bf16[2,2,4,32,512]{4,3,2,1,0:T(8,128)(2,1)}, bf16[256,1024]{1,0:T(8,128)(2,1)}, s32[256,128]{1,0:T(8,128)}) custom-call(s32[4]{0:T(128)} %holder.1, bf16[1024,1024]{1,0:T(8,128)(2,1)} %bitcast.8, bf16[256,1024]{1,0:T(8,128)(2,1)} %bitcast.12, bf16[1024,1024]{1,0:T(8,128)(2,1)} %bitcast.9, bf16[1024,1024]{1,0:T(8,128)(2,1)} %bitcast.10, ...), custom_call_target="tpu_custom_call" | custom-call | flops 10737418240 | bytes 9437184 | tf_op jit(solution)/shard_map/relay/pallas_call | solution.py:832
  89.7 0.0 copy-start
  89.7 1.0 %copy-done = bf16[2,2,4,32,512]{4,3,2,1,0:T(8,128)(2,1)S(1)} copy-done((bf16[2,2,4,32,512]{4,3,2,1,0:T(8,128)(2,1)S(1)}, bf16[2,2,4,32,512]{4,3,2,1,0:T(8,128)(2,1)}, u32[]{:S(2)}) %copy-start) | copy-done | bytes 524312
  90.7 0.0 copy-start.1
  90.7 1.0 %copy-done.1 = bf16[256,1024]{1,0:T(8,128)(2,1)S(1)} copy-done((bf16[256,1024]{1,0:T(8,128)(2,1)S(1)}, bf16[256,1024]{1,0:T(8,128)(2,1)}, u32[]{:S(2)}) %copy-start.1) | copy-done | bytes 524312
  91.8 0.0 copy-start.2
  91.8 0.9 copy-done.2
  92.7 2.7 %owner_sums.1 = (f32[1024,1024]{1,0:T(8,128)}, f32[32,1024]{1,0:T(8,128)}, f32[32,1024]{1,0:T(8,128)}) custom-call(s32[256,128]{1,0:T(8,128)S(1)} %copy-done.2, bf16[256,1024]{1,0:T(8,128)(2,1)S(1)} %copy-done.1, bf16[2,2,4,32,512]{4,3,2,1,0:T(8,128)(2,1)S(1)} %copy-done), custom_call_target="tpu_custom_call" | custom-call | flops 536870912 | bytes 5242880 | tf_op jit(solution)/shard_map/owner_sums/pallas_call | solution.py:935
Async XLA Ops:
  89.7 1.0 %copy-start = (bf16[2,2,4,32,512]{4,3,2,1,0:T(8,128)(2,1)S(1)}, bf16[2,2,4,32,512]{4,3,2,1,0:T(8,128)(2,1)}, u32[]{:S(2)}) copy-start(bf16[2,2,4,32,512]{4,3,2,1,0:T(8,128)(2,1)} %get-tuple-element.11.parts) | copy-start | bytes 1572868
  90.7 1.0 %copy-start.1 = (bf16[256,1024]{1,0:T(8,128)(2,1)S(1)}, bf16[256,1024]{1,0:T(8,128)(2,1)}, u32[]{:S(2)}) copy-start(bf16[256,1024]{1,0:T(8,128)(2,1)} %get-tuple-element.10.rows) | copy-start | bytes 1572868
  91.8 0.9 copy-start.2

commit v8 on v7

--- a/solution.py
+++ b/solution.py
@@ -24,6 +24,7 @@
 WIDE = 512
 CHUNKS = TOK // CHUNK
 SPLIT = CHUNK // PIECE
+DEPTH = 4
 PIECES = MICRO * TOK // PIECE
 SOON = (MICRO - 1) * PER_PLANE
 HALF = WIDTH // 2
@@ -386,8 +387,10 @@
             relay_copy(i).start()
         for k in range(1, CHUNKS):
             backward(0, k * CHUNK, CHUNK)
-            for i in range(SPLIT):
-                relay_copy(k * SPLIT + i).start()
+            for c in range(k * SPLIT, (k + 1) * SPLIT):
+                if c >= DEPTH:
+                    relay_copy(c - DEPTH).wait_send()
+                relay_copy(c).start()
         for m in range(1, MICRO):
             load_top(m).start()
 
@@ -450,6 +453,11 @@
         @pl.when(jnp.logical_not(first))
         def _():
             for c in pieces:
+
+                @pl.when(last)
+                def _(c=c):
+                    relay_copy(c - DEPTH).wait_send()
+
                 relay_copy(c).start()
 
     inner = jnp.logical_not(first | last)
@@ -485,17 +493,15 @@
             pick = jnp.where(target == rank[m], 1.0, 0.0).astype(BF16)
             ordered = jnp.dot(pick, nbuf[rows, :], preferred_element_type=F32).astype(BF16)
             sorted_rows[m] = ordered
-            for p in range(1, SECTIONS):
-                route_copy(m, p).start()
+            route_copy(m, 1).start()
+            route_copy(m, SECTIONS - 1).start()
+            if isinstance(m, int):
+                route_copy(m, 2).start()
             routed[pl.ds(pl.multiple_of(m * PER_PLANE, PER_PLANE), PER_PLANE), :] = ordered[
                 :PER_PLANE, :
             ]
 
     def micro_step(m, carry):
-        @pl.when(last & (m == 2))
-        def _():
-            pass_pool(1)
-
         @pl.when(last & (m > 0))
         def _():
             load_top(m).wait()
@@ -512,6 +518,12 @@
 
         def grad_slot(i):
             def work():
+                if i == 0:
+
+                    @pl.when(last & (m == 1))
+                    def _():
+                        pass_pool(1)
+
                 @pl.when(m > 0)
                 def _():
                     if i == 0:
@@ -597,6 +609,9 @@
             def _():
                 if n == 0:
                     soon_units()
+                if n == 1:
+                    for before in range(final):
+                        route_copy(before, 2).start()
                 if n == 2:
                     lax.fori_loop(1, SHARDS // 2, hand_soon, 0)
                 if n == 4:
@@ -722,43 +737,16 @@
     put_named = pltpu.make_async_copy(named, out_named, out_sem.at[0])
     put_named.start()
 
-    wait_all(all_ids, ids_send)
-    wait_all(soon, soon_send)
-
-    @pl.when((sec == 1) | last)
-    def _():
-        pool_copy(sec).wait_send()
-
-    @pl.when(sec == 2)
-    def _():
-        hop_copy(0).wait_send()
-        hop_copy(1).wait_send()
-
-    @pl.when(last)
-    def _():
-        pass_copy(0).wait_send()
-        pass_copy(1).wait_send()
-
-    @pl.when(jnp.logical_not(first))
-    def _():
-        def left(c, carry):
-            relay_copy(c).wait_send()
-            return carry
-
-        lax.fori_loop(0, PIECES, left, 0)
-
-    @pl.when(first)
-    def _():
-        for m in range(final):
-            for p in range(1, SECTIONS):
-                route_copy(m, p).wait_send()
-
-    for m in range(MICRO):
-        left_copy(m, act).wait_send()
-    for m in range(final):
-        right_copy(m, dz, m * TOK, TOK).wait_send()
-    right_copy(final, dz, final * TOK, tail).wait_send()
-    right_copy(final + 1, dz, final * TOK + tail, TOK - tail).wait_send()
+    put_rows = pltpu.make_async_copy(rows_buf, out_rows, out_sem.at[1])
+
+    def collect_rows():
+        wait_all(got_soon, soon_recv)
+        to_rows(got_soon, 0, SOON)
+        wait_all(got_late, late_recv)
+        to_rows(got_late, SOON, PER_PLANE)
+        put_rows.start()
+
+    pl.when(first)(collect_rows)
 
     for e in order:
         y = (py + e) % SIDE
@@ -787,12 +775,46 @@
                 else:
                     c_copy(h, e, c, core).start()
 
-    wait_all(got_soon, soon_recv)
-    to_rows(got_soon, 0, SOON)
-    wait_all(got_late, late_recv)
-    to_rows(got_late, SOON, PER_PLANE)
-    put_rows = pltpu.make_async_copy(rows_buf, out_rows, out_sem.at[1])
-    put_rows.start()
+    pl.when(jnp.logical_not(first))(collect_rows)
+
+    wait_all(all_ids, ids_send)
+    wait_all(soon, soon_send)
+
+    @pl.when((sec == 1) | last)
+    def _():
+        pool_copy(sec).wait_send()
+
+    @pl.when(sec == 2)
+    def _():
+        hop_copy(0).wait_send()
+        hop_copy(1).wait_send()
+
+    @pl.when(last)
+    def _():
+        pass_copy(0).wait_send()
+        pass_copy(1).wait_send()
+
+    @pl.when(jnp.logical_not(first))
+    def _():
+        def left(c, carry):
+            relay_copy(c).wait_send()
+            return carry
+
+        lax.fori_loop(jnp.where(last, PIECES - DEPTH, 0), PIECES, left, 0)
+
+    @pl.when(first)
+    def _():
+        for m in range(final):
+            for p in range(1, SECTIONS):
+                route_copy(m, p).wait_send()
+
+    for m in range(MICRO):
+        left_copy(m, act).wait_send()
+    for m in range(final):
+        right_copy(m, dz, m * TOK, TOK).wait_send()
+    right_copy(final, dz, final * TOK, tail).wait_send()
+    right_copy(final + 1, dz, final * TOK + tail, TOK - tail).wait_send()
+
     wait_all(late, late_send)
 
     @pl.when(first)

time: 95.6 us -> 100 us (1.046)
  Pallas kernels: 91.7 us -> 96.5 us
    pallas_call x1, Pallas kernels: 89 us -> 93.9 us  [relay(): pl.pallas_call(kernel, out_shape=(jax.ShapeDtypeStruct((2, 2, SIDE, SHARE...]
where the time goes in v8:
time: 100 us
  Pallas kernels  96.5 us (96%)
  local copies, waits for them, and re-layouts  2.98 us (3%)
    pallas_call x1, Pallas kernels, relay(): pl.pallas_call(kernel, out_shape=(jax.ShapeDtypeStruct((2, 2, SIDE, SHARE...  93.9 us
    unnamed x6, local copies, waits for them, and re-layouts  2.98 us
    pallas_call x1, Pallas kernels, owner_sums(): pl.pallas_call(table_kernel, grid=(ROWS_OWN // WIDE,), out_shape=(jax.Sha...  2.69 us

profile of v8, /device:TPU:1, one launch (start us, length us, event | category | flops | bytes accessed | tf_op | source)
XLA Modules:
  0.0 100.2 jit_solution(14904502572898469696)
XLA Ops:
  0.6 93.9 %relay.1 = (bf16[2,2,4,32,512]{4,3,2,1,0:T(8,128)(2,1)}, bf16[256,1024]{1,0:T(8,128)(2,1)}, s32[256,128]{1,0:T(8,128)}) custom-call(s32[4]{0:T(128)} %holder.1, bf16[1024,1024]{1,0:T(8,128)(2,1)} %bitcast.8, bf16[256,1024]{1,0:T(8,128)(2,1)} %bitcast.12, bf16[1024,1024]{1,0:T(8,128)(2,1)} %bitcast.9, bf16[1024,1024]{1,0:T(8,128)(2,1)} %bitcast.10, ...), custom_call_target="tpu_custom_call" | custom-call | flops 10737418240 | bytes 9437184 | tf_op jit(solution)/shard_map/relay/pallas_call | solution.py:854
  94.5 0.0 copy-start
  94.5 1.0 %copy-done = bf16[2,2,4,32,512]{4,3,2,1,0:T(8,128)(2,1)S(1)} copy-done((bf16[2,2,4,32,512]{4,3,2,1,0:T(8,128)(2,1)S(1)}, bf16[2,2,4,32,512]{4,3,2,1,0:T(8,128)(2,1)}, u32[]{:S(2)}) %copy-start) | copy-done | bytes 524312
  95.5 0.0 copy-start.1
  95.5 1.0 %copy-done.1 = bf16[256,1024]{1,0:T(8,128)(2,1)S(1)} copy-done((bf16[256,1024]{1,0:T(8,128)(2,1)S(1)}, bf16[256,1024]{1,0:T(8,128)(2,1)}, u32[]{:S(2)}) %copy-start.1) | copy-done | bytes 524312
  96.6 0.0 copy-start.2
  96.6 0.9 copy-done.2
  97.5 2.7 %owner_sums.1 = (f32[1024,1024]{1,0:T(8,128)}, f32[32,1024]{1,0:T(8,128)}, f32[32,1024]{1,0:T(8,128)}) custom-call(s32[256,128]{1,0:T(8,128)S(1)} %copy-done.2, bf16[256,1024]{1,0:T(8,128)(2,1)S(1)} %copy-done.1, bf16[2,2,4,32,512]{4,3,2,1,0:T(8,128)(2,1)S(1)} %copy-done), custom_call_target="tpu_custom_call" | custom-call | flops 536870912 | bytes 5242880 | tf_op jit(solution)/shard_map/owner_sums/pallas_call | solution.py:957
Async XLA Ops:
  94.5 1.0 %copy-start = (bf16[2,2,4,32,512]{4,3,2,1,0:T(8,128)(2,1)S(1)}, bf16[2,2,4,32,512]{4,3,2,1,0:T(8,128)(2,1)}, u32[]{:S(2)}) copy-start(bf16[2,2,4,32,512]{4,3,2,1,0:T(8,128)(2,1)} %get-tuple-element.11.parts) | copy-start | bytes 1572868
  95.5 1.0 %copy-start.1 = (bf16[256,1024]{1,0:T(8,128)(2,1)S(1)}, bf16[256,1024]{1,0:T(8,128)(2,1)}, u32[]{:S(2)}) copy-start(bf16[256,1024]{1,0:T(8,128)(2,1)} %get-tuple-element.10.rows) | copy-start | bytes 1572868
  96.6 0.9 copy-start.2

commit v9 on v8

--- a/solution.py
+++ b/solution.py
@@ -24,7 +24,6 @@
 WIDE = 512
 CHUNKS = TOK // CHUNK
 SPLIT = CHUNK // PIECE
-DEPTH = 4
 PIECES = MICRO * TOK // PIECE
 SOON = (MICRO - 1) * PER_PLANE
 HALF = WIDTH // 2
@@ -175,21 +174,32 @@
             pl.semaphore_signal(ready.at[1], inc=1, device_id=to, device_id_type=MESH)
 
     def tell_ids(m, n):
+        start, total = SPLIT * CHUNKS // 2, SPLIT * CHUNKS
+
+        def tell(k):
+            ids_copy((sh + k) % SHARDS, sh).start()
+
         if n == 0:
-
-            @pl.when(m == 0)
-            def _():
-                tell_plane()
-
-        if n == 1:
+            pl.when(m == 0)(tell_plane)
+        if n == start:
 
             @pl.when(m == 0)
             def _():
                 pl.semaphore_wait(ready.at[1], SIDE - 1)
 
-        @pl.when((m > 0) | (n > 0))
-        def _():
-            ids_copy((sh + m * SPLIT * CHUNKS + n) % SHARDS, sh).start()
+        if n >= start:
+            tell(m * total + n)
+        else:
+
+            @pl.when(m > 0)
+            def _():
+                tell(m * total + n)
+
+        if 0 < n < start:
+
+            @pl.when(m == 1)
+            def _():
+                tell(n)
 
     def pool_copy(s):
         return pltpu.make_async_remote_copy(
@@ -388,8 +398,6 @@
         for k in range(1, CHUNKS):
             backward(0, k * CHUNK, CHUNK)
             for c in range(k * SPLIT, (k + 1) * SPLIT):
-                if c >= DEPTH:
-                    relay_copy(c - DEPTH).wait_send()
                 relay_copy(c).start()
         for m in range(1, MICRO):
             load_top(m).start()
@@ -431,10 +439,6 @@
     def _():
         lax.fori_loop(0, WIDTH // 64, clear, 0)
 
-    @pl.when(last)
-    def _():
-        pass_pool(0)
-
     all_ids[sh] = ids[...]
     send_left(0)
 
@@ -453,11 +457,6 @@
         @pl.when(jnp.logical_not(first))
         def _():
             for c in pieces:
-
-                @pl.when(last)
-                def _(c=c):
-                    relay_copy(c - DEPTH).wait_send()
-
                 relay_copy(c).start()
 
     inner = jnp.logical_not(first | last)
@@ -509,6 +508,11 @@
         def forward_slot(j):
             def work():
                 if j == 0:
+
+                    @pl.when(last & (m == 1))
+                    def _():
+                        pass_pool(0)
+
                     forward_open(m + 1)
                 forward_tile(m + 1, j)
                 if j == WIDTH // TILE - 1:
@@ -518,7 +522,7 @@
 
         def grad_slot(i):
             def work():
-                if i == 0:
+                if i == 2:
 
                     @pl.when(last & (m == 1))
                     def _():
@@ -800,7 +804,7 @@
             relay_copy(c).wait_send()
             return carry
 
-        lax.fori_loop(jnp.where(last, PIECES - DEPTH, 0), PIECES, left, 0)
+        lax.fori_loop(0, PIECES, left, 0)
 
     @pl.when(first)
     def _():

time: 100 us -> 99.3 us (level)
  Pallas kernels: 96.5 us -> 95.4 us
    pallas_call x1, Pallas kernels: 93.9 us -> 92.7 us  [relay(): pl.pallas_call(kernel, out_shape=(jax.ShapeDtypeStruct((2, 2, SIDE, SHARE...]
where the time goes in v9:
time: 99.3 us; the launch traced here: 99 us
  Pallas kernels  95.4 us (96%)
  local copies, waits for them, and re-layouts  2.98 us (3%)
    pallas_call x1, Pallas kernels, relay(): pl.pallas_call(kernel, out_shape=(jax.ShapeDtypeStruct((2, 2, SIDE, SHARE...  92.7 us
    unnamed x6, local copies, waits for them, and re-layouts  2.98 us
    pallas_call x1, Pallas kernels, owner_sums(): pl.pallas_call(table_kernel, grid=(ROWS_OWN // WIDE,), out_shape=(jax.Sha...  2.68 us

profile of v9, /device:TPU:1, one launch (start us, length us, event | category | flops | bytes accessed | tf_op | source)
XLA Modules:
  0.0 99.0 jit_solution(16086624307173916542)
XLA Ops:
  0.6 92.7 %relay.1 = (bf16[2,2,4,32,512]{4,3,2,1,0:T(8,128)(2,1)}, bf16[256,1024]{1,0:T(8,128)(2,1)}, s32[256,128]{1,0:T(8,128)}) custom-call(s32[4]{0:T(128)} %holder.1, bf16[1024,1024]{1,0:T(8,128)(2,1)} %bitcast.8, bf16[256,1024]{1,0:T(8,128)(2,1)} %bitcast.12, bf16[1024,1024]{1,0:T(8,128)(2,1)} %bitcast.9, bf16[1024,1024]{1,0:T(8,128)(2,1)} %bitcast.10, ...), custom_call_target="tpu_custom_call" | custom-call | flops 10737418240 | bytes 9437184 | tf_op jit(solution)/shard_map/relay/pallas_call | solution.py:858
  93.3 0.0 copy-start
  93.4 1.0 %copy-done = bf16[2,2,4,32,512]{4,3,2,1,0:T(8,128)(2,1)S(1)} copy-done((bf16[2,2,4,32,512]{4,3,2,1,0:T(8,128)(2,1)S(1)}, bf16[2,2,4,32,512]{4,3,2,1,0:T(8,128)(2,1)}, u32[]{:S(2)}) %copy-start) | copy-done | bytes 524312
  94.4 0.0 copy-start.1
  94.4 1.0 %copy-done.1 = bf16[256,1024]{1,0:T(8,128)(2,1)S(1)} copy-done((bf16[256,1024]{1,0:T(8,128)(2,1)S(1)}, bf16[256,1024]{1,0:T(8,128)(2,1)}, u32[]{:S(2)}) %copy-start.1) | copy-done | bytes 524312
  95.4 0.0 copy-start.2
  95.4 0.9 copy-done.2
  96.3 2.7 %owner_sums.1 = (f32[1024,1024]{1,0:T(8,128)}, f32[32,1024]{1,0:T(8,128)}, f32[32,1024]{1,0:T(8,128)}) custom-call(s32[256,128]{1,0:T(8,128)S(1)} %copy-done.2, bf16[256,1024]{1,0:T(8,128)(2,1)S(1)} %copy-done.1, bf16[2,2,4,32,512]{4,3,2,1,0:T(8,128)(2,1)S(1)} %copy-done), custom_call_target="tpu_custom_call" | custom-call | flops 536870912 | bytes 5242880 | tf_op jit(solution)/shard_map/owner_sums/pallas_call | solution.py:961
Async XLA Ops:
  93.3 1.0 %copy-start = (bf16[2,2,4,32,512]{4,3,2,1,0:T(8,128)(2,1)S(1)}, bf16[2,2,4,32,512]{4,3,2,1,0:T(8,128)(2,1)}, u32[]{:S(2)}) copy-start(bf16[2,2,4,32,512]{4,3,2,1,0:T(8,128)(2,1)} %get-tuple-element.11.parts) | copy-start | bytes 1572868
  94.4 1.0 %copy-start.1 = (bf16[256,1024]{1,0:T(8,128)(2,1)S(1)}, bf16[256,1024]{1,0:T(8,128)(2,1)}, u32[]{:S(2)}) copy-start(bf16[256,1024]{1,0:T(8,128)(2,1)} %get-tuple-element.10.rows) | copy-start | bytes 1572868
  95.4 0.9 copy-start.2

commit v10 on v9

--- a/solution.py
+++ b/solution.py
@@ -743,14 +743,11 @@
 
     put_rows = pltpu.make_async_copy(rows_buf, out_rows, out_sem.at[1])
 
-    def collect_rows():
+    def collect_soon():
         wait_all(got_soon, soon_recv)
         to_rows(got_soon, 0, SOON)
-        wait_all(got_late, late_recv)
-        to_rows(got_late, SOON, PER_PLANE)
-        put_rows.start()
-
-    pl.when(first)(collect_rows)
+
+    pl.when(first)(collect_soon)
 
     for e in order:
         y = (py + e) % SIDE
@@ -779,7 +776,10 @@
                 else:
                     c_copy(h, e, c, core).start()
 
-    pl.when(jnp.logical_not(first))(collect_rows)
+    pl.when(jnp.logical_not(first))(collect_soon)
+    wait_all(got_late, late_recv)
+    to_rows(got_late, SOON, PER_PLANE)
+    put_rows.start()
 
     wait_all(all_ids, ids_send)
     wait_all(soon, soon_send)

time: 99.3 us -> 95.2 us (0.959)
  Pallas kernels: 95.4 us -> 91.3 us
    pallas_call x1, Pallas kernels: 92.7 us -> 88.6 us  [relay(): pl.pallas_call(kernel, out_shape=(jax.ShapeDtypeStruct((2, 2, SIDE, SHARE...]
where the time goes in v10:
time: 95.2 us; the launch traced here: 94.9 us
  Pallas kernels  91.3 us (96%)
  local copies, waits for them, and re-layouts  2.98 us (3%)
    pallas_call x1, Pallas kernels, relay(): pl.pallas_call(kernel, out_shape=(jax.ShapeDtypeStruct((2, 2, SIDE, SHARE...  88.6 us
    unnamed x6, local copies, waits for them, and re-layouts  2.98 us
    pallas_call x1, Pallas kernels, owner_sums(): pl.pallas_call(table_kernel, grid=(ROWS_OWN // WIDE,), out_shape=(jax.Sha...  2.69 us

profile of v10, /device:TPU:1, one launch (start us, length us, event | category | flops | bytes accessed | tf_op | source)
XLA Modules:
  0.0 94.9 jit_solution(5261881974391708368)
XLA Ops:
  0.6 88.6 %relay.1 = (bf16[2,2,4,32,512]{4,3,2,1,0:T(8,128)(2,1)}, bf16[256,1024]{1,0:T(8,128)(2,1)}, s32[256,128]{1,0:T(8,128)}) custom-call(s32[4]{0:T(128)} %holder.1, bf16[1024,1024]{1,0:T(8,128)(2,1)} %bitcast.8, bf16[256,1024]{1,0:T(8,128)(2,1)} %bitcast.12, bf16[1024,1024]{1,0:T(8,128)(2,1)} %bitcast.9, bf16[1024,1024]{1,0:T(8,128)(2,1)} %bitcast.10, ...), custom_call_target="tpu_custom_call" | custom-call | flops 10737418240 | bytes 9437184 | tf_op jit(solution)/shard_map/relay/pallas_call | solution.py:858
  89.3 0.0 copy-start
  89.3 1.0 %copy-done = bf16[2,2,4,32,512]{4,3,2,1,0:T(8,128)(2,1)S(1)} copy-done((bf16[2,2,4,32,512]{4,3,2,1,0:T(8,128)(2,1)S(1)}, bf16[2,2,4,32,512]{4,3,2,1,0:T(8,128)(2,1)}, u32[]{:S(2)}) %copy-start) | copy-done | bytes 524312
  90.3 0.0 copy-start.1
  90.3 1.0 %copy-done.1 = bf16[256,1024]{1,0:T(8,128)(2,1)S(1)} copy-done((bf16[256,1024]{1,0:T(8,128)(2,1)S(1)}, bf16[256,1024]{1,0:T(8,128)(2,1)}, u32[]{:S(2)}) %copy-start.1) | copy-done | bytes 524312
  91.4 0.0 copy-start.2
  91.4 0.9 copy-done.2
  92.3 2.7 %owner_sums.1 = (f32[1024,1024]{1,0:T(8,128)}, f32[32,1024]{1,0:T(8,128)}, f32[32,1024]{1,0:T(8,128)}) custom-call(s32[256,128]{1,0:T(8,128)S(1)} %copy-done.2, bf16[256,1024]{1,0:T(8,128)(2,1)S(1)} %copy-done.1, bf16[2,2,4,32,512]{4,3,2,1,0:T(8,128)(2,1)S(1)} %copy-done), custom_call_target="tpu_custom_call" | custom-call | flops 536870912 | bytes 5242880 | tf_op jit(solution)/shard_map/owner_sums/pallas_call | solution.py:961
Async XLA Ops:
  89.3 1.0 %copy-start = (bf16[2,2,4,32,512]{4,3,2,1,0:T(8,128)(2,1)S(1)}, bf16[2,2,4,32,512]{4,3,2,1,0:T(8,128)(2,1)}, u32[]{:S(2)}) copy-start(bf16[2,2,4,32,512]{4,3,2,1,0:T(8,128)(2,1)} %get-tuple-element.11.parts) | copy-start | bytes 1572868
  90.3 1.0 %copy-start.1 = (bf16[256,1024]{1,0:T(8,128)(2,1)S(1)}, bf16[256,1024]{1,0:T(8,128)(2,1)}, u32[]{:S(2)}) copy-start(bf16[256,1024]{1,0:T(8,128)(2,1)} %get-tuple-element.10.rows) | copy-start | bytes 1572868
  91.4 0.9 copy-start.2

commit v11 on v10

--- a/solution.py
+++ b/solution.py
@@ -44,6 +44,7 @@
     ids,
     out_parts,
     out_rows,
+    out_late,
     out_named,
     win,
     wout,
@@ -64,7 +65,6 @@
     soon,
     got_soon,
     late,
-    got_late,
     flat,
     named,
     rows_buf,
@@ -564,7 +564,7 @@
 
     def hand_late(k, carry):
         to = (sh + k) % SHARDS
-        unit_copy(late, got_late, late_send, late_recv, to, sh).start()
+        unit_copy(late, out_late, late_send, late_recv, to, sh).start()
         return carry
 
     def wait_all(ref, semaphore):
@@ -582,19 +582,20 @@
         soon[...] = flat[...].reshape(soon.shape).astype(BF16)
         got_soon[sh] = soon[sh]
 
+    def own_late():
+        return pltpu.make_async_copy(late.at[sh], out_late.at[sh], out_sem.at[4])
+
     def late_units():
         by_owner = routed[pl.ds(SOON, PER_PLANE), :].astype(F32)
         for b in range(8):
             flat[pl.ds(b, PER_PLANE, stride=8), :] = by_owner[:, b * 128 : (b + 1) * 128]
         late[...] = flat[pl.ds(0, PER_PLANE * 8), :].reshape(late.shape).astype(BF16)
-        got_late[sh] = late[sh]
-
-    def to_rows(got, start, count):
-        flat[pl.ds(0, count * 8), :] = got[...].astype(F32).reshape(count * 8, 128)
+        own_late().start()
+
+    def soon_rows():
+        flat[...] = got_soon[...].astype(F32).reshape(SOON * 8, 128)
         for b in range(8):
-            rows_buf[pl.ds(start, count), pl.ds(b * 128, 128)] = flat[
-                pl.ds(b, count, stride=8), :
-            ].astype(BF16)
+            rows_buf[:, pl.ds(b * 128, 128)] = flat[pl.ds(b, SOON, stride=8), :].astype(BF16)
 
     @pl.when(last)
     def _():
@@ -745,7 +746,8 @@
 
     def collect_soon():
         wait_all(got_soon, soon_recv)
-        to_rows(got_soon, 0, SOON)
+        soon_rows()
+        put_rows.start()
 
     pl.when(first)(collect_soon)
 
@@ -777,10 +779,6 @@
                     c_copy(h, e, c, core).start()
 
     pl.when(jnp.logical_not(first))(collect_soon)
-    wait_all(got_late, late_recv)
-    to_rows(got_late, SOON, PER_PLANE)
-    put_rows.start()
-
     wait_all(all_ids, ids_send)
     wait_all(soon, soon_send)
 
@@ -846,7 +844,8 @@
             for c in range(2):
                 c_copy(h, d, c, core).wait_send()
         c_copy(h, 0, 1 - core, core).wait_send()
-    for put in (put_named, put_rows, own_part(0), own_part(1)):
+    wait_all(out_late, late_recv)
+    for put in (put_named, put_rows, own_late(), own_part(0), own_part(1)):
         put.wait()
 
 
@@ -859,11 +858,12 @@
         kernel,
         out_shape=(
             jax.ShapeDtypeStruct((2, 2, SIDE, SHARE, HALF), BF16),
-            jax.ShapeDtypeStruct((TOK, WIDTH), BF16),
+            jax.ShapeDtypeStruct((SOON, WIDTH), BF16),
+            jax.ShapeDtypeStruct((SHARDS, 16, 128), BF16),
             jax.ShapeDtypeStruct((TOK, 128), jnp.int32),
         ),
         in_specs=[pl.BlockSpec(memory_space=pltpu.SMEM)] + [anywhere] * 5 + [vmem],
-        out_specs=(anywhere, anywhere, anywhere),
+        out_specs=(anywhere, anywhere, anywhere, anywhere),
         scratch_shapes=[
             pltpu.VMEM((WIDTH, WIDTH), BF16),
             pltpu.VMEM((WIDTH, WIDTH), BF16),
@@ -884,10 +884,9 @@
             pltpu.VMEM((SHARDS, 16 * (MICRO - 1), 128), BF16),
             pltpu.VMEM((SHARDS, 16 * (MICRO - 1), 128), BF16),
             pltpu.VMEM((SHARDS, 16, 128), BF16),
-            pltpu.VMEM((SHARDS, 16, 128), BF16),
             pltpu.VMEM((SOON * 8, 128), F32),
             pltpu.VMEM((TOK, 128), jnp.int32),
-            pltpu.VMEM((TOK, WIDTH), BF16),
+            pltpu.VMEM((SOON, WIDTH), BF16),
             pltpu.VMEM((TOK, WIDTH), BF16),
             pltpu.VMEM((tokens, WIDTH), BF16),
             pltpu.VMEM((tokens, WIDTH), BF16),
@@ -913,7 +912,7 @@
             dma((2,)),
             dma((2,)),
             dma((2,)),
-            dma((4,)),
+            dma((5,)),
             dma,
             dma,
             dma((MICRO,)),
@@ -937,8 +936,18 @@
     )(holder, saved, pooled, grad_top, w_in, w_out, ids)
 
 
-def table_kernel(named, rows, parts, table, out_in, out_out):
+def table_kernel(named, soon, late, parts, table, out_in, out_out, rows, flat):
     block = pl.program_id(0)
+
+    @pl.when(block == 0)
+    def _():
+        rows[pl.ds(0, SOON), :] = soon[...]
+        flat[...] = late[...].astype(F32).reshape(PER_PLANE * 8, 128)
+        for b in range(8):
+            rows[pl.ds(SOON, PER_PLANE), pl.ds(b * 128, 128)] = flat[
+                pl.ds(b, PER_PLANE, stride=8), :
+            ].astype(BF16)
+
     lane = lax.broadcasted_iota(jnp.int32, (TOK, WIDE), 1) + block * WIDE
     hit = jnp.where(lane == named[:, 0:1], 1.0, 0.0).astype(BF16)
     table[...] = dot_tn(hit, rows[...])
@@ -953,7 +962,7 @@
                 out[:, h * HALF : (h + 1) * HALF] = total
 
 
-def owner_sums(named, rows, parts):
+def owner_sums(named, soon, late, parts):
     def whole(shape):
         return pl.BlockSpec(shape, lambda b: (0,) * len(shape))
 
@@ -962,23 +971,27 @@
         table_kernel,
         grid=(ROWS_OWN // WIDE,),
         out_shape=(jax.ShapeDtypeStruct((ROWS_OWN, WIDTH), F32), share, share),
-        in_specs=[whole(named.shape), whole(rows.shape), whole(parts.shape)],
+        in_specs=[whole(array.shape) for array in (named, soon, late, parts)],
         out_specs=(
             pl.BlockSpec((WIDE, WIDTH), lambda b: (b, 0)),
             whole(share.shape),
             whole(share.shape),
         ),
+        scratch_shapes=[
+            pltpu.VMEM((TOK, WIDTH), BF16),
+            pltpu.VMEM((PER_PLANE * 8, 128), F32),
+        ],
         compiler_params=pltpu.CompilerParams(vmem_limit_bytes=32 * 1024 * 1024),
         cost_estimate=pl.CostEstimate(
             flops=2 * ROWS_OWN * TOK * WIDTH, bytes_accessed=5 * 2**20, transcendentals=0
         ),
         name="owner_sums",
-    )(named, rows, parts)
+    )(named, soon, late, parts)
 
 
 def local(saved, pooled, grad_top, w_in, w_out, feature_ids, holder_order):
     tokens = MICRO * TOK
-    parts, rows, named = relay(
+    parts, soon, late, named = relay(
         holder_order,
         saved.reshape(tokens, WIDTH),
         pooled.reshape(TOK, WIDTH),
@@ -987,7 +1000,7 @@
         w_out[0],
         jnp.transpose(feature_ids, (0, 2, 1)),
     )
-    table_grad, grad_in, grad_out = owner_sums(named, rows, parts)
+    table_grad, grad_in, grad_out = owner_sums(named, soon, late, parts)
     return (grad_in[None], grad_out[None], table_grad)
 
 

time: 95.2 us -> 96.2 us (1.011)
    unnamed x6 -> x8, local copies, waits for them, and re-layouts: 2.98 us -> 3.84 us
where the time goes in v11:
time: 96.2 us; the launch traced here: 95.9 us
  Pallas kernels  91.4 us (95%)
  local copies, waits for them, and re-layouts  3.84 us (4%)
    pallas_call x1, Pallas kernels, relay(): pl.pallas_call(kernel, out_shape=(jax.ShapeDtypeStruct((2, 2, SIDE, SHARE...  88.6 us
    unnamed x8, local copies, waits for them, and re-layouts  3.84 us
    pallas_call x1, Pallas kernels, owner_sums(): pl.pallas_call(table_kernel, grid=(ROWS_OWN // WIDE,), out_shape=(jax.Sha...  2.78 us

profile of v11, /device:TPU:1, one launch (start us, length us, event | category | flops | bytes accessed | tf_op | source)
XLA Modules:
  0.0 95.9 jit_solution(18406016109203357745)
XLA Ops:
  0.6 88.6 %relay.1 = (bf16[2,2,4,32,512]{4,3,2,1,0:T(8,128)(2,1)}, bf16[192,1024]{1,0:T(8,128)(2,1)}, bf16[32,16,128]{2,1,0:T(8,128)(2,1)}, s32[256,128]{1,0:T(8,128)}) custom-call(s32[4]{0:T(128)} %holder.1, bf16[1024,1024]{1,0:T(8,128)(2,1)} %bitcast.8, bf16[256,1024]{1,0:T(8,128)(2,1)} %bitcast.12, bf16[1024,1024]{1,0:T(8,128)(2,1)} %bitcast.9, ...), custom_call_target="tpu_custom_call" | custom-call | flops 10737418240 | bytes 9437184 | tf_op jit(solution)/shard_map/relay/pallas_call | solution.py:857
  89.3 0.0 copy-start
  89.3 1.0 %copy-done = bf16[2,2,4,32,512]{4,3,2,1,0:T(8,128)(2,1)S(1)} copy-done((bf16[2,2,4,32,512]{4,3,2,1,0:T(8,128)(2,1)S(1)}, bf16[2,2,4,32,512]{4,3,2,1,0:T(8,128)(2,1)}, u32[]{:S(2)}) %copy-start) | copy-done | bytes 524312
  90.3 0.0 copy-start.1
  90.3 1.0 %copy-done.1 = bf16[192,1024]{1,0:T(8,128)(2,1)S(1)} copy-done((bf16[192,1024]{1,0:T(8,128)(2,1)S(1)}, bf16[192,1024]{1,0:T(8,128)(2,1)}, u32[]{:S(2)}) %copy-start.1) | copy-done | bytes 393240
  91.3 0.0 copy-start.2
  91.3 0.9 copy-done.2
  92.2 0.0 copy-start.3
  92.2 0.9 copy-done.3
  93.1 2.8 %owner_sums.1 = (f32[1024,1024]{1,0:T(8,128)}, f32[32,1024]{1,0:T(8,128)}, f32[32,1024]{1,0:T(8,128)}) custom-call(s32[256,128]{1,0:T(8,128)S(1)} %copy-done.3, bf16[192,1024]{1,0:T(8,128)(2,1)S(1)} %copy-done.1, bf16[32,16,128]{2,1,0:T(8,128)(2,1)S(1)} %copy-done.2, bf16[2,2,4,32,512]{4,3,2,1,0:T(8,128)(2,1)S(1)} %copy-done), custom_call_target="tpu_custom_call" | custom-call | flops 536870912 | bytes 5242880 | tf_op jit(solution)/shard_map/owner_sums/pallas_call | solution.py:970
Async XLA Ops:
  89.3 1.0 %copy-start = (bf16[2,2,4,32,512]{4,3,2,1,0:T(8,128)(2,1)S(1)}, bf16[2,2,4,32,512]{4,3,2,1,0:T(8,128)(2,1)}, u32[]{:S(2)}) copy-start(bf16[2,2,4,32,512]{4,3,2,1,0:T(8,128)(2,1)} %get-tuple-element.13.parts) | copy-start | bytes 1572868
  90.3 1.0 %copy-start.1 = (bf16[192,1024]{1,0:T(8,128)(2,1)S(1)}, bf16[192,1024]{1,0:T(8,128)(2,1)}, u32[]{:S(2)}) copy-start(bf16[192,1024]{1,0:T(8,128)(2,1)} %get-tuple-element.11.soon) | copy-start | bytes 1179652
  91.3 0.9 copy-start.2
  92.2 0.9 copy-start.3

commit v12 on v10

--- a/solution.py
+++ b/solution.py
@@ -695,9 +695,8 @@
             x_copy(dx, y).start()
         if d != 0:
             send_y[d - 1] = total[:, HALF:].astype(BF16)
-    for e in order:
-        for d in (2, 1, 3):
-            y_copy(d, (px + e) % SIDE).start()
+            for e in order:
+                y_copy(d, (px + e) % SIDE).start()
     route(final)
 
     @pl.when(jnp.logical_not(first))

time: 95.2 us -> 95.1 us (level)
  no operation moved by 1% of the time
where the time goes in v12:
time: 95.1 us; the launch traced here: 94.9 us
  Pallas kernels  91.2 us (96%)
  local copies, waits for them, and re-layouts  2.98 us (3%)
    pallas_call x1, Pallas kernels, relay(): pl.pallas_call(kernel, out_shape=(jax.ShapeDtypeStruct((2, 2, SIDE, SHARE...  88.5 us
    unnamed x6, local copies, waits for them, and re-layouts  2.98 us
    pallas_call x1, Pallas kernels, owner_sums(): pl.pallas_call(table_kernel, grid=(ROWS_OWN // WIDE,), out_shape=(jax.Sha...  2.69 us

profile of v12, /device:TPU:1, one launch (start us, length us, event | category | flops | bytes accessed | tf_op | source)
XLA Modules:
  0.0 94.9 jit_solution(6539710025349285368)
XLA Ops:
  0.6 88.5 %relay.1 = (bf16[2,2,4,32,512]{4,3,2,1,0:T(8,128)(2,1)}, bf16[256,1024]{1,0:T(8,128)(2,1)}, s32[256,128]{1,0:T(8,128)}) custom-call(s32[4]{0:T(128)} %holder.1, bf16[1024,1024]{1,0:T(8,128)(2,1)} %bitcast.8, bf16[256,1024]{1,0:T(8,128)(2,1)} %bitcast.12, bf16[1024,1024]{1,0:T(8,128)(2,1)} %bitcast.9, bf16[1024,1024]{1,0:T(8,128)(2,1)} %bitcast.10, ...), custom_call_target="tpu_custom_call" | custom-call | flops 10737418240 | bytes 9437184 | tf_op jit(solution)/shard_map/relay/pallas_call | solution.py:857
  89.2 0.0 copy-start
  89.2 1.0 %copy-done = bf16[2,2,4,32,512]{4,3,2,1,0:T(8,128)(2,1)S(1)} copy-done((bf16[2,2,4,32,512]{4,3,2,1,0:T(8,128)(2,1)S(1)}, bf16[2,2,4,32,512]{4,3,2,1,0:T(8,128)(2,1)}, u32[]{:S(2)}) %copy-start) | copy-done | bytes 524312
  90.2 0.0 copy-start.1
  90.2 1.0 %copy-done.1 = bf16[256,1024]{1,0:T(8,128)(2,1)S(1)} copy-done((bf16[256,1024]{1,0:T(8,128)(2,1)S(1)}, bf16[256,1024]{1,0:T(8,128)(2,1)}, u32[]{:S(2)}) %copy-start.1) | copy-done | bytes 524312
  91.3 0.0 copy-start.2
  91.3 0.9 copy-done.2
  92.2 2.7 %owner_sums.1 = (f32[1024,1024]{1,0:T(8,128)}, f32[32,1024]{1,0:T(8,128)}, f32[32,1024]{1,0:T(8,128)}) custom-call(s32[256,128]{1,0:T(8,128)S(1)} %copy-done.2, bf16[256,1024]{1,0:T(8,128)(2,1)S(1)} %copy-done.1, bf16[2,2,4,32,512]{4,3,2,1,0:T(8,128)(2,1)S(1)} %copy-done), custom_call_target="tpu_custom_call" | custom-call | flops 536870912 | bytes 5242880 | tf_op jit(solution)/shard_map/owner_sums/pallas_call | solution.py:960
Async XLA Ops:
  89.2 1.0 %copy-start = (bf16[2,2,4,32,512]{4,3,2,1,0:T(8,128)(2,1)S(1)}, bf16[2,2,4,32,512]{4,3,2,1,0:T(8,128)(2,1)}, u32[]{:S(2)}) copy-start(bf16[2,2,4,32,512]{4,3,2,1,0:T(8,128)(2,1)} %get-tuple-element.11.parts) | copy-start | bytes 1572868
  90.2 1.0 %copy-start.1 = (bf16[256,1024]{1,0:T(8,128)(2,1)S(1)}, bf16[256,1024]{1,0:T(8,128)(2,1)}, u32[]{:S(2)}) copy-start(bf16[256,1024]{1,0:T(8,128)(2,1)} %get-tuple-element.10.rows) | copy-start | bytes 1572868
  91.3 0.9 copy-start.2
